TPU v7x, 256 devices: a whole 4x4x8 slice. The times are simulated.
256 devices in a mesh: seq: 128 (over y, z, x), head: 2 (over core).
Axes of the slice: x: 4, y: 4, z: 8, core: 2. Of those that a mesh axis runs over, the one named last changes fastest.
Arguments:
- mixer_input: bfloat16 [32768, 3584], P('seq', 'head'), may hold values from -6 to 6
- decay_rate: float32 [56, 32768], P('head', 'seq'), may hold values from 0 to 1
- state_in: bfloat16 [32768, 128], P('seq', 'head'), may hold values from -0.75 to 0.75
- state_out: bfloat16 [32768, 128], P('seq', 'head'), may hold values from -0.29882812 to 0.29882812
- skip_gain: float32 [56], P('head'), may hold values from 0.1 to 1.9
- att_queries: bfloat16 [32768, 3584], P('seq', 'head'), may hold values from -125 to 125
- att_keys: bfloat16 [32768, 3584], P('seq', 'head'), may hold values from -4.6 to 4.6
- att_values: bfloat16 [32768, 3584], P('seq', 'head'), may hold values from -60 to 60
- checkpoint_at: int32 [128], P('seq'), may hold values from 0 to 32767, as said below
- checkpoint_owner: int32 [128, 128], P('seq'), may hold values from 0 to 127, each once within a row
- block_owner: int32 [128, 128], P('seq'), may hold values from 0 to 127, each once within a row
Outputs:
- mixer_out: float32 [32768, 3584], P('seq', 'head')
- attention_out: bfloat16 [32768, 3584], P('seq', 'head')
- state_pool: float32 [128, 128, 1792], P('seq', None, 'head')
- cache_pool: bfloat16 [128, 256, 2, 3584], P('seq', None, None, 'head')
Inputs may be any that keep to these rules, and one draw needn't show every extreme that they name: `checkpoint_at`: checkpoint b lies among positions b * 256 to (b + 1) * 256 - 1. `checkpoint_owner`: each row names every owner once. `block_owner`: each row names every owner once.
All inputs are finite; a program needn't handle non-finite values.
Results may differ from a plain program's by a relative error of at most 0.009.
Values may be sent and summed in bfloat16 or wider, within the bound.
No kernel may reach another device: no remote copies, remote signals or barrier semaphores. Data moves between devices by JAX's collectives and lax.ppermute only.
A program may use at most 320 MiB of HBM per device.

v0:
```python
import jax
import jax.numpy as jnp
from jax import lax
from jax.sharding import PartitionSpec as P

HDIM = 64
AHDIM = 224
WIN = 2048


def entering(shard, axis, combine, identity):
    length, position = (lax.axis_size(axis), lax.axis_index(axis))
    everything = jax.tree.map(lambda part: lax.all_gather(part, axis), shard)
    start = jax.tree.map(
        lambda part, zero: jnp.broadcast_to(jnp.asarray(zero, part.dtype), part.shape),
        shard,
        identity,
    )

    def step(k, before):
        reached = k < position
        new = combine(before, jax.tree.map(lambda part: part[k], everything))
        return jax.tree.map(lambda a, b: jnp.where(reached, a, b), new, before)

    return lax.fori_loop(0, length, step, start)


def from_behind(block, axis, distance):
    devices = range(lax.axis_size(axis))
    route = [(i - distance, i) for i in devices if i - distance in devices]
    return lax.ppermute(block, axis, route)


def join_states(earlier, following):
    return (earlier[0] * following[0], following[0][:, None, None] * earlier[1] + following[1])


def absorb_block(running, query_heads, key_block, value_block, query_place, key_start, window):
    best_so_far, denom_sum, weighted = running
    key_count = key_block.shape[0]
    head_count = query_heads.shape[1]
    key_heads = key_block.reshape(key_count, head_count, -1)
    value_heads = value_block.reshape(key_count, head_count, -1)
    scale_factor = key_heads.shape[2] ** (-0.5)
    scores = (
        jnp.einsum("thd,shd->hts", query_heads, key_heads, preferred_element_type=jnp.float32)
        * scale_factor
    )
    key_place = key_start + jnp.arange(key_count, dtype=jnp.int32)
    distance = query_place[:, None] - key_place[None, :]
    allowed = ((distance >= 0) & (distance < window) & (key_place[None, :] >= 0))[None]
    masked = jnp.where(allowed, scores, -1e30)
    new_best = jnp.maximum(best_so_far, jnp.max(masked, axis=2))
    weights = jnp.where(allowed, jnp.exp(masked - new_best[:, :, None]), 0.0)
    shrink = jnp.exp(best_so_far - new_best)
    denom_sum = denom_sum * shrink + jnp.sum(weights, axis=2)
    product = jnp.einsum(
        "hts,shd->thd",
        weights.astype(jnp.bfloat16),
        value_heads,
        preferred_element_type=jnp.float32,
    )
    weighted = weighted * shrink.T[:, :, None] + product
    return (new_best, denom_sum, weighted)


def body(
    mixer_input,
    decay_rate,
    state_in,
    state_out,
    skip_gain,
    att_queries,
    att_keys,
    att_values,
    checkpoint_at,
    checkpoint_owner,
    block_owner,
):
    position = lax.axis_index("seq")
    owners = lax.axis_size("seq")
    tokens = mixer_input.shape[0]
    head_count = decay_rate.shape[0]
    mix_heads = mixer_input.reshape(tokens, head_count, HDIM)
    log_decay = jnp.cumsum(-decay_rate, axis=1)
    gram_matrix = jnp.dot(state_out, state_in.T, preferred_element_type=jnp.float32)
    later_rows = jnp.arange(tokens)[:, None] >= jnp.arange(tokens)[None, :]
    spread = jnp.where(later_rows[None], log_decay[:, :, None] - log_decay[:, None, :], 0.0)
    decay_mat = jnp.where(later_rows[None], jnp.exp(spread), 0.0)
    mix_weights = (gram_matrix[None] * decay_mat).astype(jnp.bfloat16)
    inner_part = jnp.einsum(
        "hts,shp->thp", mix_weights, mix_heads, preferred_element_type=jnp.float32
    )
    to_end = jnp.exp(log_decay[:, -1:] - log_decay)
    scaled_end = (mix_heads.astype(jnp.float32) * to_end.T[:, :, None]).astype(jnp.bfloat16)
    local_end = jnp.einsum("thp,tn->hpn", scaled_end, state_in, preferred_element_type=jnp.float32)
    block_decay = jnp.exp(log_decay[:, -1])
    identity = (jnp.ones_like(block_decay), jnp.zeros_like(local_end))
    prefix = entering((block_decay, local_end), "seq", join_states, identity)
    arriving = prefix[1]
    carried = jnp.einsum(
        "tn,hpn->thp", state_out.astype(jnp.float32), arriving, precision=lax.Precision.HIGHEST
    )
    carried = carried * jnp.exp(log_decay).T[:, :, None]
    mixer_out = (
        inner_part + carried + skip_gain[None, :, None] * mix_heads.astype(jnp.float32)
    ).reshape(tokens, -1)
    local_spot = checkpoint_at[0] - position * tokens
    spot_log = lax.dynamic_slice_in_dim(log_decay, local_spot, 1, 1)
    before_spot = (jnp.arange(tokens, dtype=jnp.int32) <= local_spot)[None, :]
    to_spot = jnp.where(
        before_spot, jnp.exp(jnp.where(before_spot, spot_log - log_decay, 0.0)), 0.0
    )
    scaled_spot = (mix_heads.astype(jnp.float32) * to_spot.T[:, :, None]).astype(jnp.bfloat16)
    spot_state = jnp.exp(spot_log)[:, :, None] * arriving + jnp.einsum(
        "thp,tn->hpn", scaled_spot, state_in, preferred_element_type=jnp.float32
    )
    owner_slots = jnp.arange(owners, dtype=jnp.int32)
    state_pick = (checkpoint_owner[0][None, :] == owner_slots[:, None]).astype(jnp.float32)
    state_pieces = spot_state.reshape(owners, -1)
    state_send = jnp.dot(state_pick, state_pieces, precision=lax.Precision.HIGHEST)
    state_pool = lax.all_to_all(state_send, "seq", split_axis=0, concat_axis=0, tiled=True)[None]
    block_len = tokens // owners
    kv_pick = (block_owner[0][None, :] == owner_slots[:, None]).astype(jnp.bfloat16)
    paired = jnp.stack(
        [att_keys.reshape(owners, block_len, -1), att_values.reshape(owners, block_len, -1)], axis=2
    )
    kv_send = (
        jnp.dot(kv_pick, paired.reshape(owners, -1), preferred_element_type=jnp.float32)
        .astype(jnp.bfloat16)
        .reshape(paired.shape)
    )
    kv_arrived = lax.all_to_all(kv_send, "seq", split_axis=0, concat_axis=0, tiled=True)
    cache_pool = kv_arrived.reshape(1, owners * block_len, 2, -1)
    query_heads = att_queries.reshape(tokens, -1, AHDIM)
    att_heads = query_heads.shape[1]
    query_place = position * tokens + jnp.arange(tokens, dtype=jnp.int32)
    initial = (
        jnp.full((att_heads, tokens), -1e30, jnp.float32),
        jnp.zeros((att_heads, tokens), jnp.float32),
        jnp.zeros((tokens, att_heads, AHDIM), jnp.float32),
    )
    running = absorb_block(
        initial, query_heads, att_keys, att_values, query_place, position * tokens, WIN
    )
    span_blocks = WIN // tokens

    def cycle_turn(turn_index, moving):
        arrived = from_behind((moving[0], moving[1]), "seq", 1)
        updated = absorb_block(
            moving[2],
            query_heads,
            arrived[0],
            arrived[1],
            query_place,
            (position - turn_index - 1) * tokens,
            WIN,
        )
        return (arrived[0], arrived[1], updated)

    finished = lax.fori_loop(0, span_blocks, cycle_turn, (att_keys, att_values, running))
    running = finished[2]
    attention_out = (running[2] / running[1].T[:, :, None]).astype(jnp.bfloat16).reshape(tokens, -1)
    return (mixer_out, attention_out, state_pool, cache_pool)


def solution(mesh):
    placed = (
        P("seq", "head"),
        P("head", "seq"),
        P("seq", "head"),
        P("seq", "head"),
        P("head"),
        P("seq", "head"),
        P("seq", "head"),
        P("seq", "head"),
        P("seq"),
        P("seq", None),
        P("seq", None),
    )
    return jax.shard_map(
        body,
        mesh=mesh,
        in_specs=placed,
        out_specs=(
            P("seq", "head"),
            P("seq", "head"),
            P("seq", None, "head"),
            P("seq", None, None, "head"),
        ),
        check_vma=False,
    )
```

profile of v0, /device:TPU:24, one launch (start us, length us, event | category | flops | bytes accessed | tf_op | source)
XLA Modules:
  0.0 1311.1 jit_solution(16186308952369592719)
XLA Ops:
  9.7 1.5 copy.59
  16.1 4.2 pad_maximum_fusion
  20.3 3.8 copy.67
  24.1 2.1 convolution_convert_fusion
  26.3 2.3 reshape.261
  28.5 16.2 %all-to-all-start.1 = ((bf16[128,2,2,1792]{3,2,1,0:T(2,128)(2,1)}), bf16[128,2,2,1792]{3,2,1,0:T(2,128)(2,1)}, u32[]{:S(2)}, u32[]{:S(2)}) async-start(bf16[128,2,2,1792]{3,2,1,0:T(2,128)(2,1)} %reshape.261), calls=%async_computation.1 | async-start | bytes 3670016 | tf_op jit(solution)/shard_map/all_to_all | solution.py:133
  50.2 657.6 %all-reduce = f32[3584]{0:T(1024)S(1)} all-reduce(f32[3584]{0:T(1024)S(1)} %dynamic-update-slice), channel_id=2, replica_groups=mesh['seq'=128,'head'=2] {'seq'}, use_global_device_ids=true, to_apply=%add | all-reduce | flops 3584 | bytes 28672
  708.1 2.0 fusion.24
  711.3 2.0 bitcast_add_fusion.2
  713.3 306.8 %while.38 = (s32[]{:T(128)}, bf16[256,1792]{0,1:T(8,128)(2,1)}, bf16[256,1792]{0,1:T(8,128)(2,1)}, f32[8,256]{1,0:T(8,128)S(1)}, f32[8,256]{1,0:T(8,128)S(1)}, /...) while((s32[]{:T(128)}, bf16[256,1792]{0,1:T(8,128)(2,1)}, ...), condition=%wide.region_9.10_spmd.clone, body=%wide.region_6.9_spmd.clone.sunk | while | flops 477830144 | bytes 38802220 | solution.py:161
  713.3 1.9 collective-permute-start
  715.2 2.2 collective-permute-start.1
  717.6 25.2 %collective-permute-done = bf16[256,1792]{0,1:T(8,128)(2,1)S(1)} collective-permute-done((bf16[256,1792]{0,1:T(8,128)(2,1)}, bf16[256,1792]{0,1:T(8,128)(2,1)S(1)}, u32[]{:S(2)}, u32[]{:S(2)}) %collective-permute-start) | collective-permute-done | bytes 917536 | tf_op jit(solution)/shard_map/while/body/eval_jaxpr/ppermute | solution.py:31
  742.9 1.8 fusion.82
  745.2 8.8 collective-permute-done.1
  757.0 1.9 collective-permute-start
  758.9 1.9 collective-permute-start.1
  761.0 25.6 %collective-permute-done = bf16[256,1792]{0,1:T(8,128)(2,1)S(1)} collective-permute-done((bf16[256,1792]{0,1:T(8,128)(2,1)}, bf16[256,1792]{0,1:T(8,128)(2,1)S(1)}, u32[]{:S(2)}, u32[]{:S(2)}) %collective-permute-start) | collective-permute-done | bytes 917536 | tf_op jit(solution)/shard_map/while/body/eval_jaxpr/ppermute | solution.py:31
  786.6 1.8 fusion.82
  789.0 7.9 collective-permute-done.1
  799.8 1.9 collective-permute-start
  801.7 1.9 collective-permute-start.1
  803.9 25.1 %collective-permute-done = bf16[256,1792]{0,1:T(8,128)(2,1)S(1)} collective-permute-done((bf16[256,1792]{0,1:T(8,128)(2,1)}, bf16[256,1792]{0,1:T(8,128)(2,1)S(1)}, u32[]{:S(2)}, u32[]{:S(2)}) %collective-permute-start) | collective-permute-done | bytes 917536 | tf_op jit(solution)/shard_map/while/body/eval_jaxpr/ppermute | solution.py:31
  828.9 1.8 fusion.82
  831.3 7.5 collective-permute-done.1
  841.7 1.9 collective-permute-start
  843.6 1.9 collective-permute-start.1
  845.7 24.2 %collective-permute-done = bf16[256,1792]{0,1:T(8,128)(2,1)S(1)} collective-permute-done((bf16[256,1792]{0,1:T(8,128)(2,1)}, bf16[256,1792]{0,1:T(8,128)(2,1)S(1)}, u32[]{:S(2)}, u32[]{:S(2)}) %collective-permute-start) | collective-permute-done | bytes 917536 | tf_op jit(solution)/shard_map/while/body/eval_jaxpr/ppermute | solution.py:31
  869.9 1.8 fusion.82
  872.2 7.5 collective-permute-done.1
  882.7 1.9 collective-permute-start
  884.6 1.9 collective-permute-start.1
  886.7 23.2 %collective-permute-done = bf16[256,1792]{0,1:T(8,128)(2,1)S(1)} collective-permute-done((bf16[256,1792]{0,1:T(8,128)(2,1)}, bf16[256,1792]{0,1:T(8,128)(2,1)S(1)}, u32[]{:S(2)}, u32[]{:S(2)}) %collective-permute-start) | collective-permute-done | bytes 917536 | tf_op jit(solution)/shard_map/while/body/eval_jaxpr/ppermute | solution.py:31
  909.9 1.8 fusion.82
  912.3 7.5 collective-permute-done.1
  922.7 1.9 collective-permute-start
  924.6 1.9 collective-permute-start.1
  926.7 15.7 %collective-permute-done = bf16[256,1792]{0,1:T(8,128)(2,1)S(1)} collective-permute-done((bf16[256,1792]{0,1:T(8,128)(2,1)}, bf16[256,1792]{0,1:T(8,128)(2,1)S(1)}, u32[]{:S(2)}, u32[]{:S(2)}) %collective-permute-start) | collective-permute-done | bytes 917536 | tf_op jit(solution)/shard_map/while/body/eval_jaxpr/ppermute | solution.py:31
  942.4 1.8 fusion.82
  944.8 7.5 collective-permute-done.1
  955.2 1.9 collective-permute-start
  957.1 1.9 collective-permute-start.1
  959.2 15.7 %collective-permute-done = bf16[256,1792]{0,1:T(8,128)(2,1)S(1)} collective-permute-done((bf16[256,1792]{0,1:T(8,128)(2,1)}, bf16[256,1792]{0,1:T(8,128)(2,1)S(1)}, u32[]{:S(2)}, u32[]{:S(2)}) %collective-permute-start) | collective-permute-done | bytes 917536 | tf_op jit(solution)/shard_map/while/body/eval_jaxpr/ppermute | solution.py:31
  974.9 1.8 fusion.82
  977.2 7.5 collective-permute-done.1
  987.7 1.9 collective-permute-start
  989.6 1.9 collective-permute-start.1
  991.7 15.7 %collective-permute-done = bf16[256,1792]{0,1:T(8,128)(2,1)S(1)} collective-permute-done((bf16[256,1792]{0,1:T(8,128)(2,1)}, bf16[256,1792]{0,1:T(8,128)(2,1)S(1)}, u32[]{:S(2)}, u32[]{:S(2)}) %collective-permute-start) | collective-permute-done | bytes 917536 | tf_op jit(solution)/shard_map/while/body/eval_jaxpr/ppermute | solution.py:31
  1007.4 1.8 fusion.82
  1009.7 7.5 collective-permute-done.1
  1020.1 2.6 divide_convert_fusion
  1022.7 182.2 %while.39 = (s32[]{:T(128)}, f32[28,64,64]{2,1,0:T(8,128)S(1)}, s32[]{:T(128)}, f32[128,28]{1,0:T(8,128)S(1)}, f32[128,28,64,64]{3,2,1,0:T(8,128)}, /*index=5*/s32[]{:T(128)}, s32[]{:T(128)}) while((s32[]{:T(128)}, f32[28,64,64]{2,1,0:T(8,128)S(1)}, s32[]{:T(128)}, f32[128,28]{1,0:T(8,128)S(1)}, f32[128,28,64,64]{3,2,1,0:T(8,128)}, ...), condition=%wide.region_3.4_spmd.clone, body=%wide.region_2.3_spmd.clone.sunk | while | flops 458756 | bytes 1376697 | solution.py:25
  1022.7 1.5 fusion.85
  1025.6 1.4 fusion.85
  1027.1 1.4 fusion.85
  1038.5 1.4 fusion.85
  1039.9 1.4 fusion.85
  1041.3 1.4 fusion.85
  1207.3 79.8 %all-to-all-start = ((f32[128,1,896]{2,1,0:T(1,128)}), f32[128,1,896]{2,1,0:T(1,128)S(1)}, u32[]{:S(2)}, u32[]{:S(2)}) async-start(f32[128,1,896]{2,1,0:T(1,128)} %copy.66), calls=%async_computation | async-start | bytes 917504 | tf_op jit(solution)/shard_map/all_to_all | solution.py:122
  1289.1 2.8 fusion.18
  1292.0 2.2 fusion.26
  1294.1 2.7 copy.68
  1296.9 2.6 all-to-all-done
  1300.3 4.0 copy.101
  (437 shorter events, 216.6 us)
Async XLA Ops:
  7.2 703.5 %copy-start = (bf16[256,64]{0,1:T(8,128)(2,1)S(1)}, bf16[256,64]{0,1:T(8,128)(2,1)}, u32[]{:S(2)}) copy-start(bf16[256,64]{0,1:T(8,128)(2,1)} %param.18) | copy-start | bytes 98308
  7.2 5.0 copy-start.12
  7.2 1015.5 %all-gather.4.cloned.1.call-start = ((), (), s32[]{:S(2)}) async-start(), calls=%async_computation.2 | async-start | bytes 118358016 | tf_op jit(solution)/shard_map/all_gather | solution.py:13
  9.7 3.9 copy-start.5
  11.2 3.6 copy-start.3
  12.1 2.7 copy-start.7
  20.3 3.8 copy-start.16
  28.5 16.2 %copy-start.6 = (bf16[256,1792]{1,0:T(8,128)(2,1)S(1)}, bf16[256,1792]{1,0:T(8,128)(2,1)}, u32[]{:S(2)}) copy-start(bf16[256,1792]{1,0:T(8,128)(2,1)} %param.21) | copy-start | bytes 2752516
  28.5 17.5 %copy-start.8 = (bf16[256,1792]{1,0:T(8,128)(2,1)S(1)}, bf16[256,1792]{1,0:T(8,128)(2,1)}, u32[]{:S(2)}) copy-start(bf16[256,1792]{1,0:T(8,128)(2,1)} %param.22) | copy-start | bytes 2752516
  28.5 1178.7 %all-to-all-start.1 = ((bf16[128,2,2,1792]{3,2,1,0:T(2,128)(2,1)}), bf16[128,2,2,1792]{3,2,1,0:T(2,128)(2,1)}, u32[]{:S(2)}, u32[]{:S(2)}) async-start(bf16[128,2,2,1792]{3,2,1,0:T(2,128)(2,1)} %reshape.261), calls=%async_computation.1 | async-start | bytes 3670016 | tf_op jit(solution)/shard_map/all_to_all | solution.py:133
  44.7 2.6 copy-start.10
  46.1 2.6 copy-start.17
  710.1 1.2 copy-start.11
  713.3 29.6 %collective-permute-start = (bf16[256,1792]{0,1:T(8,128)(2,1)}, bf16[256,1792]{0,1:T(8,128)(2,1)S(1)}, u32[]{:S(2)}, u32[]{:S(2)}) collective-permute-start(bf16[256,1792]{0,1:T(8,128)(2,1)} %get-tuple-element.590), channel_id=1, source_target_pairs={{0,2},{2,4},{4,6},{6,8},{8,10},{10,12},{12,14},{14,16},{16,18},{18... | collective-permute-start | bytes 2752520 | tf_op jit(solution)/shard_map/while/body/eval_jaxpr/ppermute | solution.py:31
  715.2 38.9 %collective-permute-start.1 = (bf16[256,1792]{0,1:T(8,128)(2,1)}, bf16[256,1792]{0,1:T(8,128)(2,1)S(1)}, u32[]{:S(2)}, u32[]{:S(2)}) collective-permute-start(bf16[256,1792]{0,1:T(8,128)(2,1)} %get-tuple-element.591), channel_id=1, source_target_pairs={{0,2},{2,4},{4,6},{6,8},{8,10},{10,12},{12,14},{14,16},{16,18},{18... | collective-permute-start | bytes 2752520 | tf_op jit(solution)/shard_map/while/body/eval_jaxpr/ppermute | solution.py:31
  744.7 9.4 copy-start.1
  755.1 1.9 copy-start.2
  757.0 29.6 %collective-permute-start = (bf16[256,1792]{0,1:T(8,128)(2,1)}, bf16[256,1792]{0,1:T(8,128)(2,1)S(1)}, u32[]{:S(2)}, u32[]{:S(2)}) collective-permute-start(bf16[256,1792]{0,1:T(8,128)(2,1)} %get-tuple-element.590), channel_id=1, source_target_pairs={{0,2},{2,4},{4,6},{6,8},{8,10},{10,12},{12,14},{14,16},{16,18},{18... | collective-permute-start | bytes 2752520 | tf_op jit(solution)/shard_map/while/body/eval_jaxpr/ppermute | solution.py:31
  758.9 37.9 %collective-permute-start.1 = (bf16[256,1792]{0,1:T(8,128)(2,1)}, bf16[256,1792]{0,1:T(8,128)(2,1)S(1)}, u32[]{:S(2)}, u32[]{:S(2)}) collective-permute-start(bf16[256,1792]{0,1:T(8,128)(2,1)} %get-tuple-element.591), channel_id=1, source_target_pairs={{0,2},{2,4},{4,6},{6,8},{8,10},{10,12},{12,14},{14,16},{16,18},{18... | collective-permute-start | bytes 2752520 | tf_op jit(solution)/shard_map/while/body/eval_jaxpr/ppermute | solution.py:31
  788.4 8.5 copy-start.1
  797.9 1.9 copy-start.2
  799.8 29.1 %collective-permute-start = (bf16[256,1792]{0,1:T(8,128)(2,1)}, bf16[256,1792]{0,1:T(8,128)(2,1)S(1)}, u32[]{:S(2)}, u32[]{:S(2)}) collective-permute-start(bf16[256,1792]{0,1:T(8,128)(2,1)} %get-tuple-element.590), channel_id=1, source_target_pairs={{0,2},{2,4},{4,6},{6,8},{8,10},{10,12},{12,14},{14,16},{16,18},{18... | collective-permute-start | bytes 2752520 | tf_op jit(solution)/shard_map/while/body/eval_jaxpr/ppermute | solution.py:31
  801.7 37.0 %collective-permute-start.1 = (bf16[256,1792]{0,1:T(8,128)(2,1)}, bf16[256,1792]{0,1:T(8,128)(2,1)S(1)}, u32[]{:S(2)}, u32[]{:S(2)}) collective-permute-start(bf16[256,1792]{0,1:T(8,128)(2,1)} %get-tuple-element.591), channel_id=1, source_target_pairs={{0,2},{2,4},{4,6},{6,8},{8,10},{10,12},{12,14},{14,16},{16,18},{18... | collective-permute-start | bytes 2752520 | tf_op jit(solution)/shard_map/while/body/eval_jaxpr/ppermute | solution.py:31
  830.7 8.1 copy-start.1
  839.8 1.9 copy-start.2
  841.7 28.2 %collective-permute-start = (bf16[256,1792]{0,1:T(8,128)(2,1)}, bf16[256,1792]{0,1:T(8,128)(2,1)S(1)}, u32[]{:S(2)}, u32[]{:S(2)}) collective-permute-start(bf16[256,1792]{0,1:T(8,128)(2,1)} %get-tuple-element.590), channel_id=1, source_target_pairs={{0,2},{2,4},{4,6},{6,8},{8,10},{10,12},{12,14},{14,16},{16,18},{18... | collective-permute-start | bytes 2752520 | tf_op jit(solution)/shard_map/while/body/eval_jaxpr/ppermute | solution.py:31
  843.6 36.1 %collective-permute-start.1 = (bf16[256,1792]{0,1:T(8,128)(2,1)}, bf16[256,1792]{0,1:T(8,128)(2,1)S(1)}, u32[]{:S(2)}, u32[]{:S(2)}) collective-permute-start(bf16[256,1792]{0,1:T(8,128)(2,1)} %get-tuple-element.591), channel_id=1, source_target_pairs={{0,2},{2,4},{4,6},{6,8},{8,10},{10,12},{12,14},{14,16},{16,18},{18... | collective-permute-start | bytes 2752520 | tf_op jit(solution)/shard_map/while/body/eval_jaxpr/ppermute | solution.py:31
  871.7 8.1 copy-start.1
  880.7 1.9 copy-start.2
  882.7 27.3 %collective-permute-start = (bf16[256,1792]{0,1:T(8,128)(2,1)}, bf16[256,1792]{0,1:T(8,128)(2,1)S(1)}, u32[]{:S(2)}, u32[]{:S(2)}) collective-permute-start(bf16[256,1792]{0,1:T(8,128)(2,1)} %get-tuple-element.590), channel_id=1, source_target_pairs={{0,2},{2,4},{4,6},{6,8},{8,10},{10,12},{12,14},{14,16},{16,18},{18... | collective-permute-start | bytes 2752520 | tf_op jit(solution)/shard_map/while/body/eval_jaxpr/ppermute | solution.py:31
  884.6 35.2 %collective-permute-start.1 = (bf16[256,1792]{0,1:T(8,128)(2,1)}, bf16[256,1792]{0,1:T(8,128)(2,1)S(1)}, u32[]{:S(2)}, u32[]{:S(2)}) collective-permute-start(bf16[256,1792]{0,1:T(8,128)(2,1)} %get-tuple-element.591), channel_id=1, source_target_pairs={{0,2},{2,4},{4,6},{6,8},{8,10},{10,12},{12,14},{14,16},{16,18},{18... | collective-permute-start | bytes 2752520 | tf_op jit(solution)/shard_map/while/body/eval_jaxpr/ppermute | solution.py:31
  911.7 8.1 copy-start.1
  920.8 1.9 copy-start.2
  922.7 19.7 %collective-permute-start = (bf16[256,1792]{0,1:T(8,128)(2,1)}, bf16[256,1792]{0,1:T(8,128)(2,1)S(1)}, u32[]{:S(2)}, u32[]{:S(2)}) collective-permute-start(bf16[256,1792]{0,1:T(8,128)(2,1)} %get-tuple-element.590), channel_id=1, source_target_pairs={{0,2},{2,4},{4,6},{6,8},{8,10},{10,12},{12,14},{14,16},{16,18},{18... | collective-permute-start | bytes 2752520 | tf_op jit(solution)/shard_map/while/body/eval_jaxpr/ppermute | solution.py:31
  924.6 27.6 %collective-permute-start.1 = (bf16[256,1792]{0,1:T(8,128)(2,1)}, bf16[256,1792]{0,1:T(8,128)(2,1)S(1)}, u32[]{:S(2)}, u32[]{:S(2)}) collective-permute-start(bf16[256,1792]{0,1:T(8,128)(2,1)} %get-tuple-element.591), channel_id=1, source_target_pairs={{0,2},{2,4},{4,6},{6,8},{8,10},{10,12},{12,14},{14,16},{16,18},{18... | collective-permute-start | bytes 2752520 | tf_op jit(solution)/shard_map/while/body/eval_jaxpr/ppermute | solution.py:31
  944.2 8.1 copy-start.1
  953.3 1.9 copy-start.2
  955.2 19.7 %collective-permute-start = (bf16[256,1792]{0,1:T(8,128)(2,1)}, bf16[256,1792]{0,1:T(8,128)(2,1)S(1)}, u32[]{:S(2)}, u32[]{:S(2)}) collective-permute-start(bf16[256,1792]{0,1:T(8,128)(2,1)} %get-tuple-element.590), channel_id=1, source_target_pairs={{0,2},{2,4},{4,6},{6,8},{8,10},{10,12},{12,14},{14,16},{16,18},{18... | collective-permute-start | bytes 2752520 | tf_op jit(solution)/shard_map/while/body/eval_jaxpr/ppermute | solution.py:31
  957.1 27.6 %collective-permute-start.1 = (bf16[256,1792]{0,1:T(8,128)(2,1)}, bf16[256,1792]{0,1:T(8,128)(2,1)S(1)}, u32[]{:S(2)}, u32[]{:S(2)}) collective-permute-start(bf16[256,1792]{0,1:T(8,128)(2,1)} %get-tuple-element.591), channel_id=1, source_target_pairs={{0,2},{2,4},{4,6},{6,8},{8,10},{10,12},{12,14},{14,16},{16,18},{18... | collective-permute-start | bytes 2752520 | tf_op jit(solution)/shard_map/while/body/eval_jaxpr/ppermute | solution.py:31
  976.7 8.1 copy-start.1
  985.7 1.9 copy-start.2
  987.7 19.7 %collective-permute-start = (bf16[256,1792]{0,1:T(8,128)(2,1)}, bf16[256,1792]{0,1:T(8,128)(2,1)S(1)}, u32[]{:S(2)}, u32[]{:S(2)}) collective-permute-start(bf16[256,1792]{0,1:T(8,128)(2,1)} %get-tuple-element.590), channel_id=1, source_target_pairs={{0,2},{2,4},{4,6},{6,8},{8,10},{10,12},{12,14},{14,16},{16,18},{18... | collective-permute-start | bytes 2752520 | tf_op jit(solution)/shard_map/while/body/eval_jaxpr/ppermute | solution.py:31
  989.6 27.6 %collective-permute-start.1 = (bf16[256,1792]{0,1:T(8,128)(2,1)}, bf16[256,1792]{0,1:T(8,128)(2,1)S(1)}, u32[]{:S(2)}, u32[]{:S(2)}) collective-permute-start(bf16[256,1792]{0,1:T(8,128)(2,1)} %get-tuple-element.591), channel_id=1, source_target_pairs={{0,2},{2,4},{4,6},{6,8},{8,10},{10,12},{12,14},{14,16},{16,18},{18... | collective-permute-start | bytes 2752520 | tf_op jit(solution)/shard_map/while/body/eval_jaxpr/ppermute | solution.py:31
  1009.1 8.1 copy-start.1
  1018.2 1.9 copy-start.2
  1022.7 182.2 %copy-start.4 = (bf16[256,1792]{0,1:T(8,128)(2,1)S(1)}, bf16[256,1792]{0,1:T(8,128)(2,1)}, u32[]{:S(2)}) copy-start(bf16[256,1792]{0,1:T(8,128)(2,1)} %copy-done.3) | copy-start | bytes 2752516
  1204.9 0.7 copy-start.14
  1205.6 82.1 %copy-start.9 = (bf16[256,8,224]{0,2,1:T(8,128)(2,1)S(1)}, bf16[256,8,224]{0,2,1:T(8,128)(2,1)}, u32[]{:S(2)}) copy-start(bf16[256,8,224]{0,2,1:T(8,128)(2,1)} %divide_convert_fusion) | copy-start | bytes 2752516
  1207.3 92.2 %all-to-all-start = ((f32[128,1,896]{2,1,0:T(1,128)}), f32[128,1,896]{2,1,0:T(1,128)S(1)}, u32[]{:S(2)}, u32[]{:S(2)}) async-start(f32[128,1,896]{2,1,0:T(1,128)} %copy.66), calls=%async_computation | async-start | bytes 917504 | tf_op jit(solution)/shard_map/all_to_all | solution.py:122
  1289.1 2.8 copy-start.13
  1289.1 2.8 copy-start.15
Sparse Core Ops, SparseCore 0:
  13.6 585.2 all-gather.3
where the time goes:
time: 1320 us; the launch traced here: 1310 us
  blocking collectives  658 us (50%)
  waiting for transfers between devices  235 us (18%)
  other arithmetic  193 us (15%)
  starting transfers between devices  127 us (10%)
  local copies, waits for them, and re-layouts  42.9 us (3%)
  matrix products  35.7 us (3%)
  between operations  15.7 us (1%)
    unnamed x1, blocking collectives  658 us
    ppermute x16, waiting for transfers between devices, from_behind(): return lax.ppermute(block, axis, route)  232 us
    select_n x128, other arithmetic, step(): return jax.tree.map(lambda a, b: jnp.where(reached, a, b), new, before)  177 us
    all_to_all x1, starting transfers between devices, body(): lax.all_to_all(state_send, 'seq', split_axis=0, concat_axis=0, tiled=True)  79.8 us
    ppermute x16, starting transfers between devices, from_behind(): return lax.ppermute(block, axis, route)  31 us
  transfers between devices with their start and end apart: 19, of which 17 were waited for; matrix products, arithmetic and copies ran while one was open for 20% of the time, Pallas kernels for 0%

commit v1 on v0

v1 whole, which is shorter than its diff:
```python
import functools

import jax
import jax.numpy as jnp
from jax import lax
from jax.experimental import pallas as pl
from jax.experimental.pallas import tpu as pltpu
from jax.sharding import PartitionSpec as P

HDIM = 64
NSTATE = 64
AHDIM = 224
TOK = 256
ROW = 4
PACK = AHDIM + 16
SCALE = AHDIM**-0.5 * 1.4426950408889634
LOWEST = -1e30
HEAVY = 4 * 10**10
BF = jnp.bfloat16
F32 = jnp.float32
HIGHEST = lax.Precision.HIGHEST


def call(kernel, out_shape, in_smem, *args, name, scratch=(), after=(), mib=16, flops=0):
    specs = [
        pl.BlockSpec(memory_space=pltpu.SMEM if i in in_smem else pltpu.VMEM)
        for i in range(len(args))
    ] + [pl.BlockSpec(memory_space=pl.ANY)] * len(after)

    def run(*refs):
        kernel(*refs[: len(args)], *refs[len(args) + len(after) :])

    outs = jax.tree.map(lambda _: pl.BlockSpec(memory_space=pltpu.VMEM), out_shape)
    return pl.pallas_call(
        run,
        out_shape=out_shape,
        in_specs=specs,
        out_specs=outs,
        scratch_shapes=list(scratch),
        compiler_params=pltpu.CompilerParams(vmem_limit_bytes=mib * 2**20),
        cost_estimate=pl.CostEstimate(flops=flops, bytes_accessed=0, transcendentals=0),
        name=name,
    )(*args, *after)


def shape(*dims, dtype=BF):
    return jax.ShapeDtypeStruct(dims, dtype)


def turn(x_ref, turned):
    for start in range(0, x_ref.shape[1], 128):
        turned[start : start + 128, :] = x_ref[:, start : start + 128].T


def pair_rows(turned, pair, odd):
    at = pair * (2 * AHDIM) + odd * AHDIM
    return turned[pl.ds(pl.multiple_of(at, 32), AHDIM), :]


def prep_kernel(place_ref, q_ref, k_ref, v_ref, *refs):
    outputs, (q, k, v) = refs[:ROW], refs[ROW:]
    for x_ref, turned in ((k_ref, k), (v_ref, v), (q_ref, q)):
        turn(x_ref, turned)
    for d in range(ROW):
        pair = lax.rem(place_ref[0] + d, ROW)
        for i, (turned, odd) in enumerate(((k, 0), (v, 0), (q, 1), (q, 0), (k, 1), (v, 1))):
            outputs[d][i * AHDIM : (i + 1) * AHDIM, :] = pair_rows(turned, pair, odd)


def gather_kernel(place_ref, *refs):
    kv_ref, q_ref, second_ref = refs[ROW:]
    for d in range(ROW):
        block = lax.rem(place_ref[0] + ROW - d, ROW)
        kv_ref[block] = refs[d][0 : 2 * AHDIM, :]
        q_ref[block] = refs[d][2 * AHDIM : 3 * AHDIM, :]
        second_ref[block] = refs[d][3 * AHDIM : 6 * AHDIM, :]


def absorb(q, keys, values, mode, qb, state):
    if mode == "causal":
        blocks = range(0, qb + 1)
    elif mode == "tail":
        blocks = range(qb, ROW)
    else:
        blocks = range(ROW)
    scores = []
    for kb in blocks:
        s = lax.dot_general(keys(kb), q, (((0,), (0,)), ((), ())), preferred_element_type=F32)
        if kb == qb and mode != "full":
            s_at = lax.broadcasted_iota(jnp.int32, s.shape, 0)
            t_at = lax.broadcasted_iota(jnp.int32, s.shape, 1)
            s = jnp.where(s_at <= t_at if mode == "causal" else s_at > t_at, s, LOWEST)
        scores.append(s)
    best = functools.reduce(jnp.maximum, [jnp.max(s, axis=0, keepdims=True) for s in scores])
    if state is not None:
        best = jnp.maximum(best, state[0])
    total, product = 0.0, 0.0
    for kb, s in zip(blocks, scores):
        p = jnp.exp2((s - best) * SCALE)
        if kb == qb and mode == "tail":
            s_at = lax.broadcasted_iota(jnp.int32, s.shape, 0)
            t_at = lax.broadcasted_iota(jnp.int32, s.shape, 1)
            p = jnp.where(s_at > t_at, p, 0.0)
        total = total + jnp.sum(p, axis=0, keepdims=True)
        product = product + jnp.dot(values(kb), p.astype(BF), preferred_element_type=F32)
    if state is not None:
        shrink = jnp.exp2((state[0] - best) * SCALE)
        total = total + state[1] * shrink
        product = product + state[2] * shrink
    return best, total, product


def rows_of(ref, first):
    return lambda kb: ref[kb, first : first + AHDIM, :]


def store_state(state, stat_ref, acc_ref, qb):
    stat_ref[qb, 0:1, :] = state[0]
    stat_ref[qb, 1:2, :] = state[1]
    acc_ref[qb] = state[2]


def load_state(stat_ref, acc_ref, qb):
    return stat_ref[qb, 0:1, :], stat_ref[qb, 1:2, :], acc_ref[qb]


def parts_of(x):
    high = x.astype(BF).astype(F32)
    rest = x - high
    middle = rest.astype(BF).astype(F32)
    return high, middle, (rest - middle).astype(BF).astype(F32)


def store_packed(state, ref, qb):
    best, total, product = state
    ref[qb, 0:AHDIM, :] = (product / jnp.where(total > 0.0, total, 1.0)).astype(BF)
    row = lax.broadcasted_iota(jnp.int32, (16, TOK), 0)
    stats = jnp.zeros((16, TOK), F32)
    for i, part in enumerate(parts_of(best) + parts_of(total)):
        stats = jnp.where(row == i, part, stats)
    ref[qb, AHDIM:PACK, :] = stats.astype(BF)


def merge_packed(state, ref, qb):
    stats = ref[qb, AHDIM:PACK, :].astype(F32)
    best = stats[0:1] + stats[1:2] + stats[2:3]
    total = stats[3:4] + stats[4:5] + stats[5:6]
    best = jnp.where(total > 0.0, best, LOWEST)
    top = jnp.maximum(best, state[0])
    other = jnp.exp2((best - top) * SCALE) * total
    mine = jnp.exp2((state[0] - top) * SCALE)
    product = state[2] * mine + ref[qb, 0:AHDIM, :].astype(F32) * other
    return top, state[1] * mine + other, product


def own_kernel(kv_ref, q_ref, second_ref, a_stat, a_acc, b_stat, b_acc):
    for qb in range(ROW):
        state = absorb(
            second_ref[qb, 0:AHDIM, :],
            rows_of(kv_ref, 0),
            rows_of(kv_ref, AHDIM),
            "causal",
            qb,
            None,
        )
        store_state(state, a_stat, a_acc, qb)
        state = absorb(
            q_ref[qb],
            rows_of(second_ref, AHDIM),
            rows_of(second_ref, 2 * AHDIM),
            "causal",
            qb,
            None,
        )
        store_state(state, b_stat, b_acc, qb)


def nearer_kernel(row_ref, second_ref, kv_ref, stat_in, acc_in, stat_ref, acc_ref):
    stat_ref[...] = stat_in[...]
    acc_ref[...] = acc_in[...]

    @pl.when(row_ref[0] >= 1)
    def _():
        for qb in range(ROW):
            state = absorb(
                second_ref[qb, 0:AHDIM, :],
                rows_of(kv_ref, 0),
                rows_of(kv_ref, AHDIM),
                "full",
                qb,
                load_state(stat_in, acc_in, qb),
            )
            store_state(state, stat_ref, acc_ref, qb)


def next_kernel(q_ref, second_ref, stat_ref, acc_ref):
    for qb in range(ROW):
        state = absorb(
            q_ref[qb],
            rows_of(second_ref, AHDIM),
            rows_of(second_ref, 2 * AHDIM),
            "full",
            qb,
            None,
        )
        store_state(state, stat_ref, acc_ref, qb)


def after_kernel(q_ref, second_ref, packed_ref):
    for qb in range(ROW):
        state = absorb(
            q_ref[qb],
            rows_of(second_ref, AHDIM),
            rows_of(second_ref, 2 * AHDIM),
            "tail",
            qb,
            None,
        )
        store_packed(state, packed_ref, qb)


def join_kernel(stat_in, acc_in, packed_in, packed_ref):
    for qb in range(ROW):
        store_packed(merge_packed(load_state(stat_in, acc_in, qb), packed_in, qb), packed_ref, qb)


def last_kernel(
    row_ref, place_ref, second_ref, kv_ref, a_stat, a_acc, b_stat, b_acc, packed_in, *refs
):
    out_ref = refs[ROW]
    for qb in range(ROW):
        _, total, product = merge_packed(load_state(b_stat, b_acc, qb), packed_in, qb)
        out_ref[qb, AHDIM : 2 * AHDIM, :] = (product / total).astype(BF)
        _, total, product = load_state(a_stat, a_acc, qb)
        out_ref[qb, 0:AHDIM, :] = (product / total).astype(BF)

    @pl.when(row_ref[0] >= 2)
    def _():
        for qb in range(ROW):
            _, total, product = absorb(
                second_ref[qb, 0:AHDIM, :],
                rows_of(kv_ref, 0),
                rows_of(kv_ref, AHDIM),
                "tail",
                qb,
                load_state(a_stat, a_acc, qb),
            )
            out_ref[qb, 0:AHDIM, :] = (product / total).astype(BF)

    for d in range(ROW):
        refs[d][...] = out_ref[lax.rem(place_ref[0] + d, ROW)]


def back_kernel(place_ref, *refs):
    out_ref, turned = refs[ROW:]
    for d in range(ROW):
        pair = lax.rem(place_ref[0] + ROW - d, ROW)
        at = pl.multiple_of(pair * (2 * AHDIM), 32)
        turned[pl.ds(at, 2 * AHDIM), :] = refs[d][...]
    for start in range(0, turned.shape[0], 128):
        out_ref[:, start : start + 128] = turned[start : start + 128, :].T


def blocks_kernel(owner_ref, k_ref, v_ref, state_ref, send_ref, slots):
    owners = owner_ref.shape[1]
    pieces = k_ref.shape[1] // 128
    rows = 4 * pieces + 8
    owner = lax.broadcasted_iota(jnp.int32, (owners, owners), 0)
    pick = (owner_ref[...] == owner).astype(BF)
    block = lax.broadcasted_iota(jnp.int32, (owners, 2 * owners), 0)
    at = lax.broadcasted_iota(jnp.int32, (owners, 2 * owners), 1)
    for i in range(2):
        places = jnp.dot(pick, (at == 2 * block + i).astype(BF), preferred_element_type=F32)
        places = places.astype(BF)
        for kind, ref in enumerate((k_ref, v_ref)):
            picked = jnp.dot(places, ref[...], preferred_element_type=F32)
            for j in range(pieces):
                slots[pl.ds((i * pieces + j) * 2 + kind, owners, stride=rows), :] = picked[
                    :, j * 128 : (j + 1) * 128
                ]
    for device in range(owners):
        slots[device * rows + 4 * pieces : (device + 1) * rows, :] = state_ref[
            device * 8 : (device + 1) * 8, :
        ]
    send_ref[...] = slots[...].astype(BF)


def expand(x, heads):
    head = lax.broadcasted_iota(jnp.int32, (heads, heads * HDIM), 0)
    column = lax.broadcasted_iota(jnp.int32, (heads, heads * HDIM), 1)
    hot = (column // HDIM == head).astype(F32)
    return jnp.dot(x, hot, precision=HIGHEST, preferred_element_type=F32)


def state_kernel(x_ref, rate_ref, write_ref, cum_ref, turned_ref, slots):
    heads = rate_ref.shape[0]
    half = heads // 2 * HDIM
    rate = rate_ref[...]
    first = lax.broadcasted_iota(jnp.int32, (TOK, TOK), 0)
    second = lax.broadcasted_iota(jnp.int32, (TOK, TOK), 1)
    cum_ref[...] = -jnp.dot(
        rate, (first <= second).astype(F32), precision=HIGHEST, preferred_element_type=F32
    )
    turned = -lax.dot_general(
        (second <= first).astype(F32),
        rate,
        (((1,), (1,)), ((), ())),
        precision=HIGHEST,
        preferred_element_type=F32,
    )
    turned_ref[...] = turned
    end = turned[TOK - 1 : TOK, :]
    scaled = (x_ref[...].astype(F32) * expand(jnp.exp(end - turned), heads)).astype(BF)
    local = lax.dot_general(
        write_ref[...], scaled, (((0,), (0,)), ((), ())), preferred_element_type=F32
    )
    for side in range(2):
        for k in range(half // 128):
            start = side * half + k * 128
            slots[pl.ds(side * NSTATE * 8 + k, NSTATE, stride=8), :] = local[:, start : start + 128]
    lane = lax.broadcasted_iota(jnp.int32, (heads, 128), 1)
    head = lax.broadcasted_iota(jnp.int32, (heads, 128), 0)
    for side in range(2):
        tail = jnp.zeros((1, 128), F32)
        for i, part in enumerate(parts_of(end)):
            hot = (lane == 3 * (head - side * (heads // 2)) + i) & (head // (heads // 2) == side)
            tail = tail + jnp.dot(
                part, hot.astype(F32), precision=HIGHEST, preferred_element_type=F32
            )
        slots[pl.ds(side * NSTATE * 8 + half // 128, NSTATE, stride=8), :] = jnp.broadcast_to(
            tail, (NSTATE, 128)
        )


def scan_kernel(got_ref, out_ref, state, decay):
    blocks = state.shape[0] // 8
    rows = got_ref.shape[0] // blocks
    for b in range(blocks):
        state[b * 8 : (b + 1) * 8, :] = got_ref[(b + 1) * rows - 16 : (b + 1) * rows, :].astype(
            F32
        )[8:16]
    tail = state[pl.ds(7, blocks, stride=8), :].astype(BF)
    part = lax.broadcasted_iota(jnp.int32, (128, 128), 0)
    column = lax.broadcasted_iota(jnp.int32, (128, 128), 1)
    for k in range(7):
        hot = (part // 3 == 2 * k + column // HDIM).astype(BF)
        decay[pl.ds(k, blocks, stride=8), :] = jnp.exp(
            jnp.dot(tail, hot, preferred_element_type=F32)
        )
    decay[pl.ds(7, blocks, stride=8), :] = jnp.zeros((blocks, 128), F32)

    def step(b, carry):
        at = pl.ds(pl.multiple_of(b * 8, 8), 8)
        after = decay[at, :] * carry + state[at, :]
        state[at, :] = carry
        return after

    lax.fori_loop(0, blocks, step, jnp.zeros((8, 128), F32), unroll=8)
    out_ref[...] = state[...].astype(BF)


def cache_kernel(got_ref, out_ref, slots):
    blocks = out_ref.shape[0]
    pieces = out_ref.shape[3] // 128
    rows = 4 * pieces + 8
    for k in range(blocks // 8):
        slots[k * 8 : (k + 1) * 8] = (
            got_ref[k * 8 * rows : (k + 1) * 8 * rows, :].astype(F32).reshape(8, rows, 128)
        )
    for i in range(2):
        for j in range(pieces):
            at = (i * pieces + j) * 2
            out_ref[:, i, :, j * 128 : (j + 1) * 128] = slots[:, at : at + 2, :].astype(BF)


def inner_kernel(
    spot_ref, x_ref, cum_ref, turned_ref, write_ref, read_ref, gain_ref, out_ref, spot_ref_out
):
    heads = cum_ref.shape[0]
    write = write_ref[...]
    turned = turned_ref[...]
    gram = lax.dot_general(
        read_ref[...], write, (((1,), (1,)), ((), ())), preferred_element_type=F32
    )
    t_at = lax.broadcasted_iota(jnp.int32, (TOK, TOK), 0)
    s_at = lax.broadcasted_iota(jnp.int32, (TOK, TOK), 1)
    later = t_at >= s_at
    left = lax.broadcasted_iota(jnp.int32, (TOK, 2 * HDIM), 1) < HDIM
    gain = expand(gain_ref[...], heads)
    for pair in range(heads // 2):
        columns = slice(pair * 2 * HDIM, (pair + 1) * 2 * HDIM)
        x = x_ref[:, columns]
        inner = []
        for h in (2 * pair, 2 * pair + 1):
            spread = jnp.where(later, turned[:, h : h + 1] - cum_ref[h : h + 1, :], LOWEST)
            weights = (gram * jnp.exp(spread)).astype(BF)
            inner.append(jnp.dot(weights, x, preferred_element_type=F32))
        out_ref[:, columns] = jnp.where(left, inner[0], inner[1]) + gain[:, columns] * x.astype(
            F32
        )
    spot = spot_ref[0]
    position = lax.broadcasted_iota(jnp.int32, (TOK, heads), 0)
    to_spot = jnp.exp(jnp.where(position <= spot, spot_log(turned, spot) - turned, LOWEST))
    scaled = (x_ref[...].astype(F32) * expand(to_spot, heads)).astype(BF)
    spot_ref_out[...] = lax.dot_general(
        write, scaled, (((0,), (0,)), ((), ())), preferred_element_type=F32
    )


def spot_log(turned, spot):
    position = lax.broadcasted_iota(jnp.int32, turned.shape, 0)
    return jnp.sum(jnp.where(position == spot, turned, 0.0), axis=0, keepdims=True)


def mixer_kernel(
    spot_ref,
    owner_ref,
    turned_ref,
    read_ref,
    inner_ref,
    local_ref,
    came_ref,
    out_ref,
    send_ref,
    slots,
    rows,
    flat,
):
    heads = turned_ref.shape[1]
    half = heads // 2 * HDIM
    turned = turned_ref[...]
    slots[...] = came_ref[...].astype(F32)
    arriving = jnp.concatenate(
        [
            slots[pl.ds(side * NSTATE * 8 + k, NSTATE, stride=8), :]
            for side in range(2)
            for k in range(half // 128)
        ],
        axis=1,
    )
    carried = jnp.dot(read_ref[...], arriving.astype(BF), preferred_element_type=F32)
    out_ref[...] = inner_ref[...] + carried * expand(jnp.exp(turned), heads)
    at_spot = expand(jnp.exp(spot_log(turned, spot_ref[0])), heads)
    state = arriving * at_spot + local_ref[...]
    rows[:, 0:NSTATE] = state.T
    even = rows[pl.ds(0, heads * HDIM // 2, stride=2), :]
    odd = pltpu.roll(rows[pl.ds(1, heads * HDIM // 2, stride=2), :], NSTATE, 1)
    lane = lax.broadcasted_iota(jnp.int32, even.shape, 1)
    flat[0 : heads * HDIM // 2, :] = jnp.where(lane < NSTATE, even, odd)
    for piece in range(owner_ref.shape[1]):
        at = pl.multiple_of(owner_ref[0, piece] * 8, 8)
        slots[pl.ds(at, 8), :] = flat[7 * piece : 7 * piece + 8, :]
    send_ref[...] = slots[...].astype(BF)


def pool_kernel(got_ref, out_ref, slots):
    slots[...] = got_ref[...].astype(F32)
    blocks = out_ref.shape[1]
    for k in range(7):
        out_ref[0, :, k * 128 : (k + 1) * 128] = slots[pl.ds(k, blocks, stride=8), :]


def to_all(x):
    return lax.all_to_all(x, "seq", split_axis=0, concat_axis=0, tiled=True)


def in_row(parts):
    count = lax.axis_size("seq")
    return [parts[0]] + [
        lax.ppermute(
            parts[d],
            "seq",
            [(i, i // ROW * ROW + (i + d) % ROW) for i in range(count)],
        )
        for d in range(1, ROW)
    ]


def shift(x, distance):
    devices = range(lax.axis_size("seq"))
    return lax.ppermute(x, "seq", [(i - distance, i) for i in devices if i - distance in devices])


def body(
    mixer_input,
    decay_rate,
    state_in,
    state_out,
    skip_gain,
    att_queries,
    att_keys,
    att_values,
    checkpoint_at,
    checkpoint_owner,
    block_owner,
):
    position = lax.axis_index("seq")
    owners = lax.axis_size("seq")
    tokens, width = mixer_input.shape
    heads = decay_rate.shape[0]
    row = (position // ROW).astype(jnp.int32)[None]

    place = (position % ROW).astype(jnp.int32)[None]
    parts = call(
        prep_kernel,
        (shape(6 * AHDIM, TOK),) * ROW,
        (0,),
        place,
        att_queries,
        att_keys,
        att_values,
        name="prep",
        scratch=[pltpu.VMEM((width, TOK), BF)] * 3,
    )
    parts = in_row(parts)

    block_len = tokens // owners
    lanes = width // 128
    cum, turned, state_send = call(
        state_kernel,
        (
            shape(heads, TOK, dtype=F32),
            shape(TOK, heads, dtype=F32),
            shape(owners * 8, 128, dtype=F32),
        ),
        (),
        mixer_input,
        decay_rate,
        state_in,
        name="state",
    )
    send = call(
        blocks_kernel,
        shape(owners * (4 * lanes + 8), 128),
        (),
        block_owner,
        att_keys,
        att_values,
        state_send,
        name="blocks",
        scratch=[pltpu.VMEM((owners * (4 * lanes + 8), 128), F32)],
        mib=24,
    )
    spot = (checkpoint_at - position * tokens).astype(jnp.int32)
    inner, spot_local = call(
        inner_kernel,
        (shape(tokens, width, dtype=F32), shape(NSTATE, width, dtype=F32)),
        (0,),
        spot,
        mixer_input,
        cum,
        turned,
        state_in,
        state_out,
        skip_gain[None, :],
        name="inner",
        after=(send,),
    )
    got = to_all(send.reshape(owners, 4 * lanes + 8, 128))
    kv_own, q_own, second = call(
        gather_kernel,
        (shape(ROW, 2 * AHDIM, TOK), shape(ROW, AHDIM, TOK), shape(ROW, 3 * AHDIM, TOK)),
        (0,),
        place,
        *parts,
        name="gather",
        after=(inner,),
    )
    kv_near = shift(kv_own, ROW)
    q_next = shift(q_own, -ROW)
    stat, acc = shape(ROW, 8, TOK, dtype=F32), shape(ROW, AHDIM, TOK, dtype=F32)
    packed = shape(ROW, PACK, TOK)
    kv_far = shift(kv_near, ROW)
    q_after = shift(q_next, -ROW)
    a_stat, a_acc, b_stat, b_acc = call(
        own_kernel, (stat, acc, stat, acc), (), kv_own, q_own, second, name="own", flops=HEAVY
    )
    n_stat, n_acc = call(
        next_kernel, (stat, acc), (), q_next, second, name="next", flops=HEAVY, after=(a_stat,)
    )
    entering = call(
        scan_kernel,
        shape(owners * 8, 128),
        (),
        got.reshape(-1, 128),
        name="scan",
        after=(n_stat,),
        scratch=[pltpu.VMEM((owners * 8, 128), F32)] * 2,
    )
    came = to_all(entering.reshape(owners, 8, 128)).reshape(owners * 8, 128)
    after = call(after_kernel, packed, (), q_after, second, name="after", flops=HEAVY, after=(n_stat,))
    after = shift(after, ROW)
    a_stat, a_acc = call(
        nearer_kernel, (stat, acc), (0,), row, second, kv_near, a_stat, a_acc, name="nearer", flops=HEAVY
    )
    join_send = call(join_kernel, packed, (), n_stat, n_acc, after, name="join", flops=HEAVY, after=(a_stat,))
    joined = shift(join_send, ROW)
    out = call(
        last_kernel,
        (shape(2 * AHDIM, TOK),) * ROW,
        (0, 1),
        row,
        place,
        second,
        kv_far,
        a_stat,
        a_acc,
        b_stat,
        b_acc,
        joined,
        name="last", flops=HEAVY,
        scratch=[pltpu.VMEM((ROW, 2 * AHDIM, TOK), BF)],
    )
    attention_out = call(
        back_kernel,
        shape(TOK, width),
        (0,),
        place,
        *in_row(out),
        name="back",
        scratch=[pltpu.VMEM((width, TOK), BF)],
    )

    mixer_out, pool_send = call(
        mixer_kernel,
        (shape(tokens, width, dtype=F32), shape(owners * 8, 128)),
        (0, 1),
        spot,
        checkpoint_owner,
        turned,
        state_out,
        inner,
        spot_local,
        came,
        name="mixer",
        after=(a_stat,),
        scratch=[
            pltpu.VMEM((owners * 8, 128), F32),
            pltpu.VMEM((width, 2 * NSTATE), F32),
            pltpu.VMEM((width // 2 + 8, 128), F32),
        ],
    )
    cache_pool = call(
        cache_kernel,
        shape(owners, block_len, 2, width),
        (),
        got.reshape(-1, 128),
        name="cache",
        scratch=[pltpu.VMEM((owners, 4 * lanes + 8, 128), F32)],
        mib=24,
        after=(pool_send,),
    ).reshape(1, owners * block_len, 2, width)
    pool_got = to_all(pool_send.reshape(owners, 8, 128)).reshape(owners * 8, 128)
    state_pool = call(
        pool_kernel,
        shape(1, owners, width // 2, dtype=F32),
        (),
        pool_got,
        name="pool",
        scratch=[pltpu.VMEM((owners * 8, 128), F32)],
    )
    return (mixer_out, attention_out, state_pool, cache_pool)


def solution(mesh):
    placed = (
        P("seq", "head"),
        P("head", "seq"),
        P("seq", "head"),
        P("seq", "head"),
        P("head"),
        P("seq", "head"),
        P("seq", "head"),
        P("seq", "head"),
        P("seq"),
        P("seq", None),
        P("seq", None),
    )
    return jax.shard_map(
        body,
        mesh=mesh,
        in_specs=placed,
        out_specs=(
            P("seq", "head"),
            P("seq", "head"),
            P("seq", None, "head"),
            P("seq", None, None, "head"),
        ),
        check_vma=False,
    )
```

time: 1320 us -> 193 us (0.15)
  blocking collectives: 658 us -> 0 us
  other arithmetic: 193 us -> 0 us
  waiting for transfers between devices: 235 us -> 57.4 us
  starting transfers between devices: 127 us -> 76.6 us
  Pallas kernels: 0 us -> 43.9 us
  matrix products: 35.7 us -> 0 us
  local copies, waits for them, and re-layouts: 42.9 us -> 12.7 us
  between operations: 15.7 us -> 1.7 us
    unnamed x1 -> x0, blocking collectives: 658 us -> none
    ppermute x16 -> x12, waiting for transfers between devices: 232 us -> 43 us  [the longest x6 30 us: shift(): lax.ppermute(x, 'seq', [(i - distance, i) for i in devices if i - distanc...]
    select_n x128 -> x0, other arithmetic: 177 us -> none  [step(): return jax.tree.map(lambda a, b: jnp.where(reached, a, b), new, before)]
    all_to_all x2 -> x3, starting transfers between devices: 96 us -> 36.3 us  [to_all(): return lax.all_to_all(x, 'seq', split_axis=0, concat_axis=0, tiled=True)]
    pallas_call x0 -> x16, Pallas kernels: none -> 43.9 us  [call(): pl.pallas_call(run, out_shape=out_shape, in_specs=specs, out_specs=outs,...]
    dot_general x25 -> x0, matrix products: 35.7 us -> none  [the longest x9 16.1 us: absorb_block(): jnp.einsum('thd,shd->hts', query_heads, key_heads, preferred_element_type...]
    while x56 -> x0, local copies, waits for them, and re-layouts: 15.4 us -> none
    ppermute x16 -> x12, starting transfers between devices: 31 us -> 40.3 us  [the longest x6 29.5 us: shift(): lax.ppermute(x, 'seq', [(i - distance, i) for i in devices if i - distanc...]
  transfers between devices with their start and end apart: 19 -> 15, of which waited for: 17 -> 8; matrix products, arithmetic and copies ran while one was open for 20% -> 1% of each run, Pallas kernels for 0% -> 21%
where the time goes in v1:
time: 193 us; the launch traced here: 192 us
  starting transfers between devices  76.6 us (40%)
  waiting for transfers between devices  57.4 us (30%)
  Pallas kernels  43.9 us (23%)
  local copies, waits for them, and re-layouts  12.7 us (7%)
    pallas_call x16, Pallas kernels, call(): pl.pallas_call(run, out_shape=out_shape, in_specs=specs, out_specs=outs,...  43.9 us
    all_to_all x3, starting transfers between devices, to_all(): return lax.all_to_all(x, 'seq', split_axis=0, concat_axis=0, tiled=True)  36.3 us
    ppermute x6, waiting for transfers between devices, shift(): lax.ppermute(x, 'seq', [(i - distance, i) for i in devices if i - distanc...  30 us
    ppermute x6, starting transfers between devices, shift(): lax.ppermute(x, 'seq', [(i - distance, i) for i in devices if i - distanc...  29.5 us
    all_to_all x3, waiting for transfers between devices, to_all(): return lax.all_to_all(x, 'seq', split_axis=0, concat_axis=0, tiled=True)  14.4 us
    ppermute x6, waiting for transfers between devices, in_row(): lax.ppermute(parts[d], 'seq', [(i, i // ROW * ROW + (i + d) % ROW) for i...  13 us
    unnamed x58, local copies, waits for them, and re-layouts  12.7 us
    ppermute x6, starting transfers between devices, in_row(): lax.ppermute(parts[d], 'seq', [(i, i // ROW * ROW + (i + d) % ROW) for i...  10.8 us
  transfers between devices with their start and end apart: 15, of which 8 were waited for; matrix products, arithmetic and copies ran while one was open for 1% of the time, Pallas kernels for 21%

profile of v1, /device:TPU:24, one launch (start us, length us, event | category | flops | bytes accessed | tf_op | source)
XLA Modules:
  0.0 192.3 jit_solution(272251621532500718)
XLA Ops:
  0.7 1.2 copy-done.2
  1.8 1.2 copy-done.4
  3.0 1.2 copy-done.7
  4.2 2.2 %prep.1 = (bf16[1344,256]{1,0:T(8,128)(2,1)S(1)}, bf16[1344,256]{1,0:T(8,128)(2,1)}, bf16[1344,256]{1,0:T(8,128)(2,1)}, bf16[1344,256]{1,0:T(8,128)(2,1)}) custom-call(s32[1]{0:T(128)} %bitcast.4.refs_0_.refs_1_, bf16[256,1792]{1,0:T(8,128)(2,1)S(1)} %copy-done.7, bf16[256,1792]{1,0:T(8,128)(2,1)S(1)} %copy-done.2, bf16[256,1792]{1,0:T(8,128)(2,1)S(1)} %copy-done.4), custom_call_target="tpu_custom_call" | custom-call | tf_op jit(solution)/shard_map/prep/pallas_call | solution.py:34
  6.4 1.5 collective-permute-start
  7.9 2.7 %collective-permute-start.1 = (bf16[1344,256]{1,0:T(8,128)(2,1)}, bf16[1344,256]{1,0:T(8,128)(2,1)}, u32[]{:S(2)}, u32[]{:S(2)}) collective-permute-start(bf16[1344,256]{1,0:T(8,128)(2,1)} %get-tuple-element.37), channel_id=1, source_target_pairs={{0,4},{2,6},{4,0},{6,2},{8,12},{10,14},{12,8},{14,10},{16,20},{18,... | collective-permute-start | bytes 2064392 | tf_op jit(solution)/shard_map/ppermute | solution.py:470
  10.7 1.4 collective-permute-start.2
  12.1 0.9 copy.15.refs_2_.refs_4_
  13.0 0.0 copy-start.15
  13.0 0.7 copy-done.15
  13.7 2.6 %state.1 = (f32[28,256]{1,0:T(8,128)S(1)}, f32[256,28]{1,0:T(8,128)S(1)}, f32[1024,128]{1,0:T(8,128)S(1)}) custom-call(bf16[256,1792]{1,0:T(8,128)(2,1)S(1)} %copy-done.6, f32[28,256]{1,0:T(8,128)S(1)} %copy-done.15, bf16[256,64]{1,0:T(8,128)(2,1)S(1)} %copy.15.refs_2_.refs_4_), custom_call_target="tpu_custom_call" | custom-call | tf_op jit(solution)/shard_map/state/pallas_call | solution.py:34
  16.3 0.7 copy-done.10
  17.0 4.3 %blocks.1.refs_7_ = bf16[8192,128]{1,0:T(8,128)(2,1)} custom-call(s32[1,128]{1,0:T(1,128)S(1)} %copy-done.16, bf16[256,1792]{1,0:T(8,128)(2,1)S(1)} %copy-done.3, bf16[256,1792]{1,0:T(8,128)(2,1)S(1)} %copy-done.5, f32[1024,128]{1,0:T(8,128)S(1)} %get-tuple-element.32.refs_3_), custom_call_target="tpu_custom_call" | custom-call | tf_op jit(solution)/shard_map/blocks/pallas_call | solution.py:34
  21.3 13.8 %all-to-all-start = ((bf16[128,64,128]{2,1,0:T(8,128)(2,1)}), bf16[128,64,128]{2,1,0:T(8,128)(2,1)}, u32[]{:S(2)}, u32[]{:S(2)}) async-start(bf16[128,64,128]{2,1,0:T(8,128)(2,1)} %bitcast.2), calls=%async_computation | async-start | bytes 4194304 | tf_op jit(solution)/shard_map/all_to_all | solution.py:464
  35.8 0.1 copy.18.refs_5_.refs_3_
  36.0 3.5 %inner.1 = (f32[256,1792]{1,0:T(8,128)S(1)}, f32[64,1792]{1,0:T(8,128)S(1)}) custom-call(s32[1]{0:T(128)S(6)} %sub.11.refs_0_, bf16[256,1792]{1,0:T(8,128)(2,1)S(1)} %copy-done.6, f32[28,256]{1,0:T(8,128)S(1)} %get-tuple-element.31.refs_2_, f32[256,28]{1,0:T(8,128)S(1)} %copy-done.11, bf16[256,64]{1,0:T(8,128)(2,1)S(1)} %copy.15.refs_2_.refs_4_, ...), custom_call_target="tpu_custom_call" | custom-call | tf_op jit(solution)/shard_map/inner/pallas_call | solution.py:34
  39.5 0.0 copy-start
  39.5 0.0 copy-start.13
  39.5 0.0 collective-permute-done.refs_2_
  39.5 5.1 %collective-permute-done.1.refs_3_ = bf16[1344,256]{1,0:T(8,128)(2,1)} collective-permute-done((bf16[1344,256]{1,0:T(8,128)(2,1)}, bf16[1344,256]{1,0:T(8,128)(2,1)}, u32[]{:S(2)}, u32[]{:S(2)}) %collective-permute-start.1) | collective-permute-done | bytes 688160 | tf_op jit(solution)/shard_map/ppermute | solution.py:470
  44.6 1.6 collective-permute-done.2.refs_4_
  46.2 1.7 gather.1
  47.9 11.6 %collective-permute-start.3 = (bf16[4,224,256]{2,1,0:T(8,128)(2,1)S(1)}, bf16[4,224,256]{2,1,0:T(8,128)(2,1)S(1)}, u32[]{:S(2)}, u32[]{:S(2)}) collective-permute-start(bf16[4,224,256]{2,1,0:T(8,128)(2,1)S(1)} %get-tuple-element.39.refs_1_), channel_id=1, source_target_pairs={{8,0},{10,2},{12,4},{14,6},{16,8},{18,10},{20,12},{22,14},{24,16},... | collective-permute-start | bytes 1376264 | tf_op jit(solution)/shard_map/ppermute | solution.py:481
  59.5 1.9 collective-permute-start.4
  61.4 3.0 %own.1 = (f32[4,8,256]{2,1,0:T(8,128)S(1)}, f32[4,224,256]{2,1,0:T(8,128)S(1)}, f32[4,8,256]{2,1,0:T(8,128)S(1)}, f32[4,224,256]{2,1,0:T(8,128)S(1)}) custom-call(bf16[4,448,256]{2,1,0:T(8,128)(2,1)S(1)} %get-tuple-element.41.refs_0_, bf16[4,224,256]{2,1,0:T(8,128)(2,1)S(1)} %get-tuple-element.39.refs_1_, ...), custom_call_target="tpu_custom_call" | custom-call | flops 40000000000 | tf_op jit(solution)/shard_map/own/pallas_call | solution.py:34
  64.4 0.9 copy-done.21
  65.3 24.2 %collective-permute-done.3.refs_0_ = bf16[4,224,256]{2,1,0:T(8,128)(2,1)S(1)} collective-permute-done((bf16[4,224,256]{2,1,0:T(8,128)(2,1)S(1)}, bf16[4,224,256]{2,1,0:T(8,128)(2,1)S(1)}, u32[]{:S(2)}, u32[]{:S(2)}) %collective-permute-start.3) | collective-permute-done | bytes 458784 | tf_op jit(solution)/shard_map/ppermute | solution.py:481
  89.6 4.9 %collective-permute-start.6 = (bf16[4,224,256]{2,1,0:T(8,128)(2,1)S(1)}, bf16[4,224,256]{2,1,0:T(8,128)(2,1)S(1)}, u32[]{:S(2)}, u32[]{:S(2)}) collective-permute-start(bf16[4,224,256]{2,1,0:T(8,128)(2,1)S(1)} %collective-permute-done.3.refs_0_), channel_id=1, source_target_pairs={{8,0},{10,2},{12,4},{14,6},{16,8},{18,10},{20,12},{22,14},{24,16},... | collective-permute-start | bytes 1376264 | tf_op jit(solution)/shard_map/ppermute | solution.py:481
  94.5 2.7 %next.1 = (f32[4,8,256]{2,1,0:T(8,128)S(1)}, f32[4,224,256]{2,1,0:T(8,128)S(1)}) custom-call(bf16[4,224,256]{2,1,0:T(8,128)(2,1)S(1)} %collective-permute-done.3.refs_0_, bf16[4,672,256]{2,1,0:T(8,128)(2,1)S(1)} %get-tuple-element.40.refs_2_.refs_1_, f32[4,8,256]{2,1,0:T(8,128)S(1)} %get-tuple-element.42.refs_2_.refs_3_), custom_call_target="tpu_custom_call" | custom-call | flops 40000000000 | tf_op jit(solution)/shard_map/next/pallas_call | solution.py:34
  97.2 0.0 copy-start.25
  97.2 5.8 %collective-permute-done.6.refs_0_ = bf16[4,224,256]{2,1,0:T(8,128)(2,1)S(1)} collective-permute-done((bf16[4,224,256]{2,1,0:T(8,128)(2,1)S(1)}, bf16[4,224,256]{2,1,0:T(8,128)(2,1)S(1)}, u32[]{:S(2)}, u32[]{:S(2)}) %collective-permute-start.6) | collective-permute-done | bytes 458784 | tf_op jit(solution)/shard_map/ppermute | solution.py:481
  102.9 1.7 after.1
  104.6 3.0 %collective-permute-start.7 = (bf16[4,240,256]{2,1,0:T(8,128)(2,1)S(1)}, bf16[4,240,256]{2,1,0:T(8,128)(2,1)S(1)}, u32[]{:S(2)}, u32[]{:S(2)}) collective-permute-start(bf16[4,240,256]{2,1,0:T(8,128)(2,1)S(1)} %after.1), channel_id=1, source_target_pairs={{0,8},{2,10},{4,12},{6,14},{8,16},{10,18},{12,20},{14,22},{16,24},... | collective-permute-start | bytes 1474568 | tf_op jit(solution)/shard_map/ppermute | solution.py:481
  107.6 0.0 collective-permute-done.4.refs_2_
  107.6 4.7 %collective-permute-start.5 = (bf16[4,448,256]{2,1,0:T(8,128)(2,1)}, bf16[4,448,256]{2,1,0:T(8,128)(2,1)}, u32[]{:S(2)}, u32[]{:S(2)}) collective-permute-start(bf16[4,448,256]{2,1,0:T(8,128)(2,1)} %collective-permute-done.4.refs_2_), channel_id=1, source_target_pairs={{0,8},{2,10},{4,12},{6,14},{8,16},{10,18},{12,20},{14,22},{16,24},... | collective-permute-start | bytes 2752520 | tf_op jit(solution)/shard_map/ppermute | solution.py:481
  112.4 4.2 %nearer.1 = (f32[4,8,256]{2,1,0:T(8,128)S(1)}, f32[4,224,256]{2,1,0:T(8,128)S(1)}) custom-call(s32[1]{0:T(128)} %bitcast.7.refs_0_, bf16[4,672,256]{2,1,0:T(8,128)(2,1)S(1)} %get-tuple-element.40.refs_2_.refs_1_, bf16[4,448,256]{2,1,0:T(8,128)(2,1)} %collective-permute-done.4.refs_2_, f32[4,8,256]{2,1,0:T(8,128)S(1)} %get-tuple-element.42.refs_2_.refs_3_, ...), custom_call_target="tpu_custom_call" | custom-call | flops 40000000000 | tf_op jit(solution)/shard_map/nearer/pallas_call | solution.py:34
  116.6 0.0 copy-start.23
  116.6 0.9 copy-done.23
  117.5 2.9 %scan.1 = bf16[1024,128]{1,0:T(8,128)(2,1)} custom-call(bf16[8192,128]{1,0:T(8,128)(2,1)} %bitcast.3.refs_0_, f32[4,8,256]{2,1,0:T(8,128)S(1)} %get-tuple-element.43.refs_1_.refs_2_.refs_0_), custom_call_target="tpu_custom_call" | custom-call | tf_op jit(solution)/shard_map/scan/pallas_call | solution.py:34
  120.4 11.7 %all-to-all-start.1 = ((bf16[128,8,128]{2,1,0:T(8,128)(2,1)}), bf16[128,8,128]{2,1,0:T(8,128)(2,1)S(1)}, u32[]{:S(2)}, u32[]{:S(2)}) async-start(bf16[128,8,128]{2,1,0:T(8,128)(2,1)} %bitcast.5), calls=%async_computation.1 | async-start | bytes 524288 | tf_op jit(solution)/shard_map/all_to_all | solution.py:464
  132.2 0.0 collective-permute-done.7.refs_2_
  132.2 0.0 copy-start.26
  132.2 1.2 copy-done.26
  133.4 0.0 copy-start.18
  133.4 1.0 join.1
  134.4 3.4 %collective-permute-start.8 = (bf16[4,240,256]{2,1,0:T(8,128)(2,1)}, bf16[4,240,256]{2,1,0:T(8,128)(2,1)S(1)}, u32[]{:S(2)}, u32[]{:S(2)}) collective-permute-start(bf16[4,240,256]{2,1,0:T(8,128)(2,1)} %join.1), channel_id=1, source_target_pairs={{0,8},{2,10},{4,12},{6,14},{8,16},{10,18},{12,20},{14,22},{16,24},... | collective-permute-start | bytes 1474568 | tf_op jit(solution)/shard_map/ppermute | solution.py:481
  137.8 14.4 %all-to-all-done.1 = bf16[128,8,128]{2,1,0:T(8,128)(2,1)S(1)} async-done(((bf16[128,8,128]{2,1,0:T(8,128)(2,1)}), bf16[128,8,128]{2,1,0:T(8,128)(2,1)S(1)}, u32[]{:S(2)}, u32[]{:S(2)}) %all-to-all-start.1) | async-done | bytes 262176 | tf_op jit(solution)/shard_map/all_to_all | solution.py:464
  152.2 4.2 %mixer.1 = (f32[256,1792]{1,0:T(8,128)}, bf16[1024,128]{1,0:T(8,128)(2,1)}) custom-call(s32[1]{0:T(128)S(6)} %sub.11.refs_0_, s32[1,128]{1,0:T(1,128)S(1)} %copy-done.18, f32[256,28]{1,0:T(8,128)S(1)} %copy-done.12, bf16[256,64]{1,0:T(8,128)(2,1)S(1)} %copy-done.9, f32[256,1792]{1,0:T(8,128)S(1)} %copy-done.1, f32[64,1792]{1,0:T(8,128)S(1)} %copy-done.14, ...), custom_call_target="tpu_custom_call" | custom-call | tf_op jit(solution)/shard_map/mixer/pallas_call | solution.py:34
  156.4 10.8 %all-to-all-start.2 = ((bf16[128,8,128]{2,1,0:T(8,128)(2,1)}), bf16[128,8,128]{2,1,0:T(8,128)(2,1)S(1)}, u32[]{:S(2)}, u32[]{:S(2)}) async-start(bf16[128,8,128]{2,1,0:T(8,128)(2,1)} %bitcast.8), calls=%async_computation.2 | async-start | bytes 524288 | tf_op jit(solution)/shard_map/all_to_all | solution.py:464
  167.2 0.0 collective-permute-done.5.refs_3_
  167.2 1.3 copy-done.20
  168.6 1.2 copy-done.22
  169.7 1.2 copy-done.24
  170.9 3.1 %last.1 = (bf16[448,256]{1,0:T(8,128)(2,1)S(1)}, bf16[448,256]{1,0:T(8,128)(2,1)S(1)}, bf16[448,256]{1,0:T(8,128)(2,1)S(1)}, bf16[448,256]{1,0:T(8,128)(2,1)S(1)}) custom-call(s32[1]{0:T(128)} %bitcast.7.refs_0_, s32[1]{0:T(128)} %bitcast.4.refs_0_.refs_1_, bf16[4,672,256]{2,1,0:T(8,128)(2,1)S(1)} %copy-done.20, ...), custom_call_target="tpu_custom_call" | custom-call | flops 40000000000 | tf_op jit(solution)/shard_map/last/pallas_call | solution.py:34
  174.0 3.1 %collective-permute-start.10 = (bf16[448,256]{1,0:T(8,128)(2,1)S(1)}, bf16[448,256]{1,0:T(8,128)(2,1)S(1)}, u32[]{:S(2)}, u32[]{:S(2)}) collective-permute-start(bf16[448,256]{1,0:T(8,128)(2,1)S(1)} %get-tuple-element.53), channel_id=1, source_target_pairs={{0,4},{2,6},{4,0},{6,2},{8,12},{10,14},{12,8},{14,10},{16,20},{18,... | collective-permute-start | bytes 688136 | tf_op jit(solution)/shard_map/ppermute | solution.py:470
  177.1 1.2 collective-permute-start.11
  178.3 0.9 collective-permute-start.9
  179.1 2.5 %collective-permute-done.10.refs_3_ = bf16[448,256]{1,0:T(8,128)(2,1)S(1)} collective-permute-done((bf16[448,256]{1,0:T(8,128)(2,1)S(1)}, bf16[448,256]{1,0:T(8,128)(2,1)S(1)}, u32[]{:S(2)}, u32[]{:S(2)}) %collective-permute-start.10) | collective-permute-done | bytes 229408 | tf_op jit(solution)/shard_map/ppermute | solution.py:470
  181.6 2.5 %collective-permute-done.11.refs_4_ = bf16[448,256]{1,0:T(8,128)(2,1)S(1)} collective-permute-done((bf16[448,256]{1,0:T(8,128)(2,1)S(1)}, bf16[448,256]{1,0:T(8,128)(2,1)S(1)}, u32[]{:S(2)}, u32[]{:S(2)}) %collective-permute-start.11) | collective-permute-done | bytes 229408 | tf_op jit(solution)/shard_map/ppermute | solution.py:470
  184.1 1.4 collective-permute-done.9.refs_2_
  185.5 1.3 back.1
  186.8 4.6 %cache.1 = bf16[128,2,2,1792]{3,2,1,0:T(2,128)(2,1)} custom-call(bf16[8192,128]{1,0:T(8,128)(2,1)} %bitcast.3.refs_0_, bf16[1024,128]{1,0:T(8,128)(2,1)} %get-tuple-element.55.refs_1_), custom_call_target="tpu_custom_call" | custom-call | tf_op jit(solution)/shard_map/cache/pallas_call | solution.py:34
  191.4 0.0 all-to-all-done.2
  191.4 0.9 pool.1
  (40 shorter events, 0.1 us)
Async XLA Ops:
  0.6 1.2 copy-start.2
  1.8 1.2 copy-start.4
  3.0 1.2 copy-start.7
  4.2 8.8 %copy-start.6 = (bf16[256,1792]{1,0:T(8,128)(2,1)S(1)}, bf16[256,1792]{1,0:T(8,128)(2,1)}, u32[]{:S(2)}) copy-start(bf16[256,1792]{1,0:T(8,128)(2,1)} %refs_1_.7) | copy-start | bytes 2752516
  4.2 12.8 %copy-start.3 = (bf16[256,1792]{1,0:T(8,128)(2,1)S(1)}, bf16[256,1792]{1,0:T(8,128)(2,1)}, u32[]{:S(2)}) copy-start(bf16[256,1792]{1,0:T(8,128)(2,1)} %refs_2_.4) | copy-start | bytes 2752516
  4.2 12.8 %copy-start.5 = (bf16[256,1792]{1,0:T(8,128)(2,1)S(1)}, bf16[256,1792]{1,0:T(8,128)(2,1)}, u32[]{:S(2)}) copy-start(bf16[256,1792]{1,0:T(8,128)(2,1)} %refs_3_.2) | copy-start | bytes 2752516
  4.2 12.8 %copy-start.16 = (s32[1,128]{1,0:T(1,128)S(1)}, s32[1,128]{1,0:T(1,128)}, u32[]{:S(2)}) copy-start(s32[1,128]{1,0:T(1,128)} %refs_0_.3) | copy-start | bytes 1540
  6.4 33.1 %collective-permute-start = (bf16[1344,256]{1,0:T(8,128)(2,1)}, bf16[1344,256]{1,0:T(8,128)(2,1)}, u32[]{:S(2)}, u32[]{:S(2)}) collective-permute-start(bf16[1344,256]{1,0:T(8,128)(2,1)} %get-tuple-element.36), channel_id=1, source_target_pairs={{0,2},{2,4},{4,6},{6,0},{8,10},{10,12},{12,14},{14,8},{16,18},{18,... | collective-permute-start | bytes 2064392 | tf_op jit(solution)/shard_map/ppermute | solution.py:470
  7.9 36.7 %collective-permute-start.1 = (bf16[1344,256]{1,0:T(8,128)(2,1)}, bf16[1344,256]{1,0:T(8,128)(2,1)}, u32[]{:S(2)}, u32[]{:S(2)}) collective-permute-start(bf16[1344,256]{1,0:T(8,128)(2,1)} %get-tuple-element.37), channel_id=1, source_target_pairs={{0,4},{2,6},{4,0},{6,2},{8,12},{10,14},{12,8},{14,10},{16,20},{18,... | collective-permute-start | bytes 2064392 | tf_op jit(solution)/shard_map/ppermute | solution.py:470
  10.7 35.5 %collective-permute-start.2 = (bf16[1344,256]{1,0:T(8,128)(2,1)}, bf16[1344,256]{1,0:T(8,128)(2,1)}, u32[]{:S(2)}, u32[]{:S(2)}) collective-permute-start(bf16[1344,256]{1,0:T(8,128)(2,1)} %get-tuple-element.38), channel_id=1, source_target_pairs={{0,6},{2,0},{4,2},{6,4},{8,14},{10,8},{12,10},{14,12},{16,22},{18,... | collective-permute-start | bytes 2064392 | tf_op jit(solution)/shard_map/ppermute | solution.py:470
  13.0 0.8 copy-start.15
  16.3 0.7 copy-start.10
  21.3 14.5 %copy-start.27 = (bf16[256,64]{0,1:T(8,128)(2,1)S(1)}, bf16[256,64]{0,1:T(8,128)(2,1)}, u32[]{:S(2)}) copy-start(bf16[256,64]{0,1:T(8,128)(2,1)} %param.14) | copy-start | bytes 98308
  21.3 14.7 %copy-start.11 = (f32[256,28]{1,0:T(8,128)S(1)}, f32[256,28]{1,0:T(8,128)}, u32[]{:S(2)}) copy-start(f32[256,28]{1,0:T(8,128)} %copy-done.10) | copy-start | bytes 86020
  21.3 14.7 %copy-start.17 = (f32[28]{0:T(128)S(1)}, f32[28]{0:T(128)}, u32[]{:S(2)}) copy-start(f32[28]{0:T(128)} %param.15) | copy-start | bytes 340
  21.3 96.2 %all-to-all-start = ((bf16[128,64,128]{2,1,0:T(8,128)(2,1)}), bf16[128,64,128]{2,1,0:T(8,128)(2,1)}, u32[]{:S(2)}, u32[]{:S(2)}) async-start(bf16[128,64,128]{2,1,0:T(8,128)(2,1)} %bitcast.2), calls=%async_computation | async-start | bytes 4194304 | tf_op jit(solution)/shard_map/all_to_all | solution.py:464
  35.9 12.0 %copy-start.8 = (bf16[256,64]{1,0:T(8,128)(2,1)}, bf16[256,64]{1,0:T(8,128)(2,1)S(1)}, u32[]{:S(2)}) copy-start(bf16[256,64]{1,0:T(8,128)(2,1)S(1)} %copy.18.refs_5_.refs_3_) | copy-start | bytes 98308
  39.5 8.4 %copy-start = (f32[256,1792]{1,0:T(8,128)}, f32[256,1792]{1,0:T(8,128)S(1)}, u32[]{:S(2)}) copy-start(f32[256,1792]{1,0:T(8,128)S(1)} %get-tuple-element.33.refs_5_.refs_4_) | copy-start | bytes 5505028
  39.5 8.4 %copy-start.13 = (f32[64,1792]{1,0:T(8,128)}, f32[64,1792]{1,0:T(8,128)S(1)}, u32[]{:S(2)}) copy-start(f32[64,1792]{1,0:T(8,128)S(1)} %get-tuple-element.34.refs_5_) | copy-start | bytes 1376260
  47.9 64.5 %copy-start.19 = (bf16[4,672,256]{2,1,0:T(8,128)(2,1)}, bf16[4,672,256]{2,1,0:T(8,128)(2,1)S(1)}, u32[]{:S(2)}) copy-start(bf16[4,672,256]{2,1,0:T(8,128)(2,1)S(1)} %get-tuple-element.40.refs_2_.refs_1_) | copy-start | bytes 4128772
  47.9 41.6 %collective-permute-start.3 = (bf16[4,224,256]{2,1,0:T(8,128)(2,1)S(1)}, bf16[4,224,256]{2,1,0:T(8,128)(2,1)S(1)}, u32[]{:S(2)}, u32[]{:S(2)}) collective-permute-start(bf16[4,224,256]{2,1,0:T(8,128)(2,1)S(1)} %get-tuple-element.39.refs_1_), channel_id=1, source_target_pairs={{8,0},{10,2},{12,4},{14,6},{16,8},{18,10},{20,12},{22,14},{24,16},... | collective-permute-start | bytes 1376264 | tf_op jit(solution)/shard_map/ppermute | solution.py:481
  59.5 48.2 %collective-permute-start.4 = (bf16[4,448,256]{2,1,0:T(8,128)(2,1)S(1)}, bf16[4,448,256]{2,1,0:T(8,128)(2,1)}, u32[]{:S(2)}, u32[]{:S(2)}) collective-permute-start(bf16[4,448,256]{2,1,0:T(8,128)(2,1)S(1)} %get-tuple-element.41.refs_0_), channel_id=1, source_target_pairs={{0,8},{2,10},{4,12},{6,14},{8,16},{10,18},{12,20},{14,22},{16,24},... | collective-permute-start | bytes 2752520 | tf_op jit(solution)/shard_map/ppermute | solution.py:481
  64.4 0.9 copy-start.21
  89.6 13.4 %collective-permute-start.6 = (bf16[4,224,256]{2,1,0:T(8,128)(2,1)S(1)}, bf16[4,224,256]{2,1,0:T(8,128)(2,1)S(1)}, u32[]{:S(2)}, u32[]{:S(2)}) collective-permute-start(bf16[4,224,256]{2,1,0:T(8,128)(2,1)S(1)} %collective-permute-done.3.refs_0_), channel_id=1, source_target_pairs={{8,0},{10,2},{12,4},{14,6},{16,8},{18,10},{20,12},{22,14},{24,16},... | collective-permute-start | bytes 1376264 | tf_op jit(solution)/shard_map/ppermute | solution.py:481
  97.2 7.5 %copy-start.25 = (f32[4,224,256]{2,1,0:T(8,128)}, f32[4,224,256]{2,1,0:T(8,128)S(1)}, u32[]{:S(2)}) copy-start(f32[4,224,256]{2,1,0:T(8,128)S(1)} %get-tuple-element.50.refs_1_) | copy-start | bytes 2752516
  104.6 27.5 %collective-permute-start.7 = (bf16[4,240,256]{2,1,0:T(8,128)(2,1)S(1)}, bf16[4,240,256]{2,1,0:T(8,128)(2,1)S(1)}, u32[]{:S(2)}, u32[]{:S(2)}) collective-permute-start(bf16[4,240,256]{2,1,0:T(8,128)(2,1)S(1)} %after.1), channel_id=1, source_target_pairs={{0,8},{2,10},{4,12},{6,14},{8,16},{10,18},{12,20},{14,22},{16,24},... | collective-permute-start | bytes 1474568 | tf_op jit(solution)/shard_map/ppermute | solution.py:481
  107.6 59.6 %collective-permute-start.5 = (bf16[4,448,256]{2,1,0:T(8,128)(2,1)}, bf16[4,448,256]{2,1,0:T(8,128)(2,1)}, u32[]{:S(2)}, u32[]{:S(2)}) collective-permute-start(bf16[4,448,256]{2,1,0:T(8,128)(2,1)} %collective-permute-done.4.refs_2_), channel_id=1, source_target_pairs={{0,8},{2,10},{4,12},{6,14},{8,16},{10,18},{12,20},{14,22},{16,24},... | collective-permute-start | bytes 2752520 | tf_op jit(solution)/shard_map/ppermute | solution.py:481
  116.6 0.9 copy-start.23
  120.4 31.7 %all-to-all-start.1 = ((bf16[128,8,128]{2,1,0:T(8,128)(2,1)}), bf16[128,8,128]{2,1,0:T(8,128)(2,1)S(1)}, u32[]{:S(2)}, u32[]{:S(2)}) async-start(bf16[128,8,128]{2,1,0:T(8,128)(2,1)} %bitcast.5), calls=%async_computation.1 | async-start | bytes 524288 | tf_op jit(solution)/shard_map/all_to_all | solution.py:464
  132.2 1.2 copy-start.26
  133.3 18.8 %copy-start.1 = (f32[256,1792]{1,0:T(8,128)S(1)}, f32[256,1792]{1,0:T(8,128)}, u32[]{:S(2)}) copy-start(f32[256,1792]{1,0:T(8,128)} %copy-done) | copy-start | bytes 5505028
  133.3 18.8 %copy-start.9 = (bf16[256,64]{1,0:T(8,128)(2,1)S(1)}, bf16[256,64]{1,0:T(8,128)(2,1)}, u32[]{:S(2)}) copy-start(bf16[256,64]{1,0:T(8,128)(2,1)} %copy-done.8) | copy-start | bytes 98308
  133.4 18.8 %copy-start.12 = (f32[256,28]{1,0:T(8,128)S(1)}, f32[256,28]{1,0:T(8,128)}, u32[]{:S(2)}) copy-start(f32[256,28]{1,0:T(8,128)} %copy-done.10) | copy-start | bytes 86020
  133.4 18.8 %copy-start.14 = (f32[64,1792]{1,0:T(8,128)S(1)}, f32[64,1792]{1,0:T(8,128)}, u32[]{:S(2)}) copy-start(f32[64,1792]{1,0:T(8,128)} %copy-done.13) | copy-start | bytes 1376260
  133.4 18.8 %copy-start.18 = (s32[1,128]{1,0:T(1,128)S(1)}, s32[1,128]{1,0:T(1,128)}, u32[]{:S(2)}) copy-start(s32[1,128]{1,0:T(1,128)} %refs_1_.9) | copy-start | bytes 1540
  134.4 32.8 %collective-permute-start.8 = (bf16[4,240,256]{2,1,0:T(8,128)(2,1)}, bf16[4,240,256]{2,1,0:T(8,128)(2,1)S(1)}, u32[]{:S(2)}, u32[]{:S(2)}) collective-permute-start(bf16[4,240,256]{2,1,0:T(8,128)(2,1)} %join.1), channel_id=1, source_target_pairs={{0,8},{2,10},{4,12},{6,14},{8,16},{10,18},{12,20},{14,22},{16,24},... | collective-permute-start | bytes 1474568 | tf_op jit(solution)/shard_map/ppermute | solution.py:481
  156.4 35.0 %all-to-all-start.2 = ((bf16[128,8,128]{2,1,0:T(8,128)(2,1)}), bf16[128,8,128]{2,1,0:T(8,128)(2,1)S(1)}, u32[]{:S(2)}, u32[]{:S(2)}) async-start(bf16[128,8,128]{2,1,0:T(8,128)(2,1)} %bitcast.8), calls=%async_computation.2 | async-start | bytes 524288 | tf_op jit(solution)/shard_map/all_to_all | solution.py:464
  167.2 1.3 copy-start.20
  168.6 1.2 copy-start.22
  169.7 1.2 copy-start.24
  174.0 7.6 %collective-permute-start.10 = (bf16[448,256]{1,0:T(8,128)(2,1)S(1)}, bf16[448,256]{1,0:T(8,128)(2,1)S(1)}, u32[]{:S(2)}, u32[]{:S(2)}) collective-permute-start(bf16[448,256]{1,0:T(8,128)(2,1)S(1)} %get-tuple-element.53), channel_id=1, source_target_pairs={{0,4},{2,6},{4,0},{6,2},{8,12},{10,14},{12,8},{14,10},{16,20},{18,... | collective-permute-start | bytes 688136 | tf_op jit(solution)/shard_map/ppermute | solution.py:470
  177.1 7.0 %collective-permute-start.11 = (bf16[448,256]{1,0:T(8,128)(2,1)S(1)}, bf16[448,256]{1,0:T(8,128)(2,1)S(1)}, u32[]{:S(2)}, u32[]{:S(2)}) collective-permute-start(bf16[448,256]{1,0:T(8,128)(2,1)S(1)} %get-tuple-element.54), channel_id=1, source_target_pairs={{0,6},{2,0},{4,2},{6,4},{8,14},{10,8},{12,10},{14,12},{16,22},{18,... | collective-permute-start | bytes 688136 | tf_op jit(solution)/shard_map/ppermute | solution.py:470
  178.3 7.2 %collective-permute-start.9 = (bf16[448,256]{1,0:T(8,128)(2,1)S(1)}, bf16[448,256]{1,0:T(8,128)(2,1)S(1)}, u32[]{:S(2)}, u32[]{:S(2)}) collective-permute-start(bf16[448,256]{1,0:T(8,128)(2,1)S(1)} %get-tuple-element.52), channel_id=1, source_target_pairs={{0,2},{2,4},{4,6},{6,0},{8,10},{10,12},{12,14},{14,8},{16,18},{18,... | collective-permute-start | bytes 688136 | tf_op jit(solution)/shard_map/ppermute | solution.py:470

commit v2 on v1

--- a/solution.py
+++ b/solution.py
@@ -16,6 +16,7 @@
 SCALE = AHDIM**-0.5 * 1.4426950408889634
 LOWEST = -1e30
 HEAVY = 4 * 10**10
+FIRST = 6
 BF = jnp.bfloat16
 F32 = jnp.float32
 HIGHEST = lax.Precision.HIGHEST
@@ -27,20 +28,26 @@
         for i in range(len(args))
     ] + [pl.BlockSpec(memory_space=pl.ANY)] * len(after)
 
+    many = isinstance(out_shape, tuple)
+    out_shapes = (out_shape if many else (out_shape,)) + (shape(8, 128, dtype=F32),)
+    first_out = len(args) + len(after)
+    token = first_out + len(out_shapes) - 1
+
     def run(*refs):
-        kernel(*refs[: len(args)], *refs[len(args) + len(after) :])
-
-    outs = jax.tree.map(lambda _: pl.BlockSpec(memory_space=pltpu.VMEM), out_shape)
-    return pl.pallas_call(
+        kernel(*refs[: len(args)], *refs[first_out:token], *refs[token + 1 :])
+        refs[token][...] = jnp.zeros((8, 128), F32)
+
+    results = pl.pallas_call(
         run,
-        out_shape=out_shape,
+        out_shape=out_shapes,
         in_specs=specs,
-        out_specs=outs,
+        out_specs=tuple(pl.BlockSpec(memory_space=pltpu.VMEM) for _ in out_shapes),
         scratch_shapes=list(scratch),
         compiler_params=pltpu.CompilerParams(vmem_limit_bytes=mib * 2**20),
         cost_estimate=pl.CostEstimate(flops=flops, bytes_accessed=0, transcendentals=0),
         name=name,
     )(*args, *after)
+    return (results[:-1] if many else results[0]), results[-1]
 
 
 def shape(*dims, dtype=BF):
@@ -85,7 +92,7 @@
         blocks = range(ROW)
     scores = []
     for kb in blocks:
-        s = lax.dot_general(keys(kb), q, (((0,), (0,)), ((), ())), preferred_element_type=F32)
+        s = jnp.dot(keys(kb), q, preferred_element_type=F32)
         if kb == qb and mode != "full":
             s_at = lax.broadcasted_iota(jnp.int32, s.shape, 0)
             t_at = lax.broadcasted_iota(jnp.int32, s.shape, 1)
@@ -114,6 +121,11 @@
     return lambda kb: ref[kb, first : first + AHDIM, :]
 
 
+def keys_of(ref, first):
+    turned = [ref[kb, first : first + AHDIM, :].T for kb in range(ROW)]
+    return lambda kb: turned[kb]
+
+
 def store_state(state, stat_ref, acc_ref, qb):
     stat_ref[qb, 0:1, :] = state[0]
     stat_ref[qb, 1:2, :] = state[1]
@@ -154,10 +166,11 @@
 
 
 def own_kernel(kv_ref, q_ref, second_ref, a_stat, a_acc, b_stat, b_acc):
+    a_keys, b_keys = keys_of(kv_ref, 0), keys_of(second_ref, AHDIM)
     for qb in range(ROW):
         state = absorb(
             second_ref[qb, 0:AHDIM, :],
-            rows_of(kv_ref, 0),
+            a_keys,
             rows_of(kv_ref, AHDIM),
             "causal",
             qb,
@@ -166,7 +179,7 @@
         store_state(state, a_stat, a_acc, qb)
         state = absorb(
             q_ref[qb],
-            rows_of(second_ref, AHDIM),
+            b_keys,
             rows_of(second_ref, 2 * AHDIM),
             "causal",
             qb,
@@ -181,10 +194,11 @@
 
     @pl.when(row_ref[0] >= 1)
     def _():
+        keys = keys_of(kv_ref, 0)
         for qb in range(ROW):
             state = absorb(
                 second_ref[qb, 0:AHDIM, :],
-                rows_of(kv_ref, 0),
+                keys,
                 rows_of(kv_ref, AHDIM),
                 "full",
                 qb,
@@ -194,10 +208,11 @@
 
 
 def next_kernel(q_ref, second_ref, stat_ref, acc_ref):
+    keys = keys_of(second_ref, AHDIM)
     for qb in range(ROW):
         state = absorb(
             q_ref[qb],
-            rows_of(second_ref, AHDIM),
+            keys,
             rows_of(second_ref, 2 * AHDIM),
             "full",
             qb,
@@ -207,10 +222,11 @@
 
 
 def after_kernel(q_ref, second_ref, packed_ref):
+    keys = keys_of(second_ref, AHDIM)
     for qb in range(ROW):
         state = absorb(
             q_ref[qb],
-            rows_of(second_ref, AHDIM),
+            keys,
             rows_of(second_ref, 2 * AHDIM),
             "tail",
             qb,
@@ -236,10 +252,11 @@
 
     @pl.when(row_ref[0] >= 2)
     def _():
+        keys = keys_of(kv_ref, 0)
         for qb in range(ROW):
             _, total, product = absorb(
                 second_ref[qb, 0:AHDIM, :],
-                rows_of(kv_ref, 0),
+                keys,
                 rows_of(kv_ref, AHDIM),
                 "tail",
                 qb,
@@ -261,10 +278,10 @@
         out_ref[:, start : start + 128] = turned[start : start + 128, :].T
 
 
-def blocks_kernel(owner_ref, k_ref, v_ref, state_ref, send_ref, slots):
+def blocks_kernel(owner_ref, k_ref, v_ref, state_ref, send_ref, later_ref, slots, later):
     owners = owner_ref.shape[1]
     pieces = k_ref.shape[1] // 128
-    rows = 4 * pieces + 8
+    rows, later_rows = slots.shape[0] // owners, later.shape[0] // owners
     owner = lax.broadcasted_iota(jnp.int32, (owners, owners), 0)
     pick = (owner_ref[...] == owner).astype(BF)
     block = lax.broadcasted_iota(jnp.int32, (owners, 2 * owners), 0)
@@ -275,14 +292,21 @@
         for kind, ref in enumerate((k_ref, v_ref)):
             picked = jnp.dot(places, ref[...], preferred_element_type=F32)
             for j in range(pieces):
-                slots[pl.ds((i * pieces + j) * 2 + kind, owners, stride=rows), :] = picked[
-                    :, j * 128 : (j + 1) * 128
-                ]
+                tile = picked[:, j * 128 : (j + 1) * 128]
+                if j < FIRST:
+                    slots[pl.ds((i * FIRST + j) * 2 + kind, owners, stride=rows), :] = tile
+                else:
+                    row = (i * (pieces - FIRST) + j - FIRST) * 2 + kind
+                    later[pl.ds(row, owners, stride=later_rows), :] = tile
     for device in range(owners):
-        slots[device * rows + 4 * pieces : (device + 1) * rows, :] = state_ref[
+        slots[(device + 1) * rows - 8 : (device + 1) * rows, :] = state_ref[
             device * 8 : (device + 1) * 8, :
         ]
+        later[(device + 1) * later_rows - 8 : (device + 1) * later_rows, :] = jnp.zeros(
+            (8, 128), F32
+        )
     send_ref[...] = slots[...].astype(BF)
+    later_ref[...] = later[...].astype(BF)
 
 
 def expand(x, heads):
@@ -311,9 +335,7 @@
     turned_ref[...] = turned
     end = turned[TOK - 1 : TOK, :]
     scaled = (x_ref[...].astype(F32) * expand(jnp.exp(end - turned), heads)).astype(BF)
-    local = lax.dot_general(
-        write_ref[...], scaled, (((0,), (0,)), ((), ())), preferred_element_type=F32
-    )
+    local = jnp.dot(write_ref[...], scaled, preferred_element_type=F32)
     for side in range(2):
         for k in range(half // 128):
             start = side * half + k * 128
@@ -359,18 +381,24 @@
     out_ref[...] = state[...].astype(BF)
 
 
-def cache_kernel(got_ref, out_ref, slots):
+def cache_kernel(got_ref, later_ref, out_ref, pool_ref, slots, later):
     blocks = out_ref.shape[0]
     pieces = out_ref.shape[3] // 128
-    rows = 4 * pieces + 8
-    for k in range(blocks // 8):
-        slots[k * 8 : (k + 1) * 8] = (
-            got_ref[k * 8 * rows : (k + 1) * 8 * rows, :].astype(F32).reshape(8, rows, 128)
-        )
+    for ref, held in ((got_ref, slots), (later_ref, later)):
+        rows = held.shape[1]
+        for k in range(blocks // 8):
+            part = ref[k * 8 * rows : (k + 1) * 8 * rows, :].astype(F32)
+            held[k * 8 : (k + 1) * 8] = part.reshape(8, rows, 128)
     for i in range(2):
         for j in range(pieces):
-            at = (i * pieces + j) * 2
-            out_ref[:, i, :, j * 128 : (j + 1) * 128] = slots[:, at : at + 2, :].astype(BF)
+            held, row = (
+                (slots, (i * FIRST + j) * 2)
+                if j < FIRST
+                else (later, (i * (pieces - FIRST) + j - FIRST) * 2)
+            )
+            out_ref[:, i, :, j * 128 : (j + 1) * 128] = held[:, row : row + 2, :].astype(BF)
+    for k in range(7):
+        pool_ref[0, :, k * 128 : (k + 1) * 128] = later[:, later.shape[1] - 8 + k, :]
 
 
 def inner_kernel(
@@ -380,7 +408,7 @@
     write = write_ref[...]
     turned = turned_ref[...]
     gram = lax.dot_general(
-        read_ref[...], write, (((1,), (1,)), ((), ())), preferred_element_type=F32
+        read_ref[...], write, (((0,), (0,)), ((), ())), preferred_element_type=F32
     )
     t_at = lax.broadcasted_iota(jnp.int32, (TOK, TOK), 0)
     s_at = lax.broadcasted_iota(jnp.int32, (TOK, TOK), 1)
@@ -402,9 +430,7 @@
     position = lax.broadcasted_iota(jnp.int32, (TOK, heads), 0)
     to_spot = jnp.exp(jnp.where(position <= spot, spot_log(turned, spot) - turned, LOWEST))
     scaled = (x_ref[...].astype(F32) * expand(to_spot, heads)).astype(BF)
-    spot_ref_out[...] = lax.dot_general(
-        write, scaled, (((0,), (0,)), ((), ())), preferred_element_type=F32
-    )
+    spot_ref_out[...] = jnp.dot(write, scaled, preferred_element_type=F32)
 
 
 def spot_log(turned, spot):
@@ -412,25 +438,10 @@
     return jnp.sum(jnp.where(position == spot, turned, 0.0), axis=0, keepdims=True)
 
 
-def mixer_kernel(
-    spot_ref,
-    owner_ref,
-    turned_ref,
-    read_ref,
-    inner_ref,
-    local_ref,
-    came_ref,
-    out_ref,
-    send_ref,
-    slots,
-    rows,
-    flat,
-):
-    heads = turned_ref.shape[1]
+def arrived(came_ref, slots, heads):
     half = heads // 2 * HDIM
-    turned = turned_ref[...]
     slots[...] = came_ref[...].astype(F32)
-    arriving = jnp.concatenate(
+    return jnp.concatenate(
         [
             slots[pl.ds(side * NSTATE * 8 + k, NSTATE, stride=8), :]
             for side in range(2)
@@ -438,26 +449,36 @@
         ],
         axis=1,
     )
-    carried = jnp.dot(read_ref[...], arriving.astype(BF), preferred_element_type=F32)
-    out_ref[...] = inner_ref[...] + carried * expand(jnp.exp(turned), heads)
-    at_spot = expand(jnp.exp(spot_log(turned, spot_ref[0])), heads)
+
+
+def mixer_kernel(turned_ref, read_ref, inner_ref, came_ref, out_ref, slots):
+    heads = turned_ref.shape[1]
+    arriving = arrived(came_ref, slots, heads).astype(BF)
+    carried = lax.dot_general(
+        read_ref[...], arriving, (((0,), (0,)), ((), ())), preferred_element_type=F32
+    )
+    out_ref[...] = inner_ref[...] + carried * expand(jnp.exp(turned_ref[...]), heads)
+
+
+def spot_kernel(
+    spot_ref, owner_ref, turned_ref, local_ref, came_ref, later_ref, send_ref, slots, rows, flat, later
+):
+    heads = turned_ref.shape[1]
+    arriving = arrived(came_ref, slots, heads)
+    at_spot = expand(jnp.exp(spot_log(turned_ref[...], spot_ref[0])), heads)
     state = arriving * at_spot + local_ref[...]
     rows[:, 0:NSTATE] = state.T
     even = rows[pl.ds(0, heads * HDIM // 2, stride=2), :]
     odd = pltpu.roll(rows[pl.ds(1, heads * HDIM // 2, stride=2), :], NSTATE, 1)
     lane = lax.broadcasted_iota(jnp.int32, even.shape, 1)
     flat[0 : heads * HDIM // 2, :] = jnp.where(lane < NSTATE, even, odd)
-    for piece in range(owner_ref.shape[1]):
-        at = pl.multiple_of(owner_ref[0, piece] * 8, 8)
-        slots[pl.ds(at, 8), :] = flat[7 * piece : 7 * piece + 8, :]
-    send_ref[...] = slots[...].astype(BF)
-
-
-def pool_kernel(got_ref, out_ref, slots):
-    slots[...] = got_ref[...].astype(F32)
-    blocks = out_ref.shape[1]
-    for k in range(7):
-        out_ref[0, :, k * 128 : (k + 1) * 128] = slots[pl.ds(k, blocks, stride=8), :]
+    later[...] = later_ref[...].astype(F32)
+    owners = owner_ref.shape[1]
+    each = later.shape[0] // owners
+    for piece in range(owners):
+        at = pl.multiple_of(owner_ref[0, piece] * each + each - 8, 8)
+        later[pl.ds(at, 8), :] = flat[7 * piece : 7 * piece + 8, :]
+    send_ref[...] = later[...].astype(BF)
 
 
 def to_all(x):
@@ -501,7 +522,7 @@
     row = (position // ROW).astype(jnp.int32)[None]
 
     place = (position % ROW).astype(jnp.int32)[None]
-    parts = call(
+    parts, _ = call(
         prep_kernel,
         (shape(6 * AHDIM, TOK),) * ROW,
         (0,),
@@ -516,7 +537,8 @@
 
     block_len = tokens // owners
     lanes = width // 128
-    cum, turned, state_send = call(
+    rows, later_rows = 4 * FIRST + 8, 4 * (lanes - FIRST) + 8
+    (cum, turned, state_send), _ = call(
         state_kernel,
         (
             shape(heads, TOK, dtype=F32),
@@ -526,23 +548,26 @@
         (),
         mixer_input,
         decay_rate,
-        state_in,
+        state_in.T,
         name="state",
     )
-    send = call(
+    (send, later), sent = call(
         blocks_kernel,
-        shape(owners * (4 * lanes + 8), 128),
+        (shape(owners * rows, 128), shape(owners * later_rows, 128)),
         (),
         block_owner,
         att_keys,
         att_values,
         state_send,
         name="blocks",
-        scratch=[pltpu.VMEM((owners * (4 * lanes + 8), 128), F32)],
+        scratch=[
+            pltpu.VMEM((owners * rows, 128), F32),
+            pltpu.VMEM((owners * later_rows, 128), F32),
+        ],
         mib=24,
     )
     spot = (checkpoint_at - position * tokens).astype(jnp.int32)
-    inner, spot_local = call(
+    (inner, spot_local), inner_done = call(
         inner_kernel,
         (shape(tokens, width, dtype=F32), shape(NSTATE, width, dtype=F32)),
         (0,),
@@ -550,52 +575,96 @@
         mixer_input,
         cum,
         turned,
-        state_in,
-        state_out,
+        state_in.T,
+        state_out.T,
         skip_gain[None, :],
         name="inner",
-        after=(send,),
-    )
-    got = to_all(send.reshape(owners, 4 * lanes + 8, 128))
-    kv_own, q_own, second = call(
+        after=(sent,),
+    )
+    got = to_all(send.reshape(owners, rows, 128)).reshape(-1, 128)
+
+    (kv_own, q_own, second), _ = call(
         gather_kernel,
         (shape(ROW, 2 * AHDIM, TOK), shape(ROW, AHDIM, TOK), shape(ROW, 3 * AHDIM, TOK)),
         (0,),
         place,
         *parts,
         name="gather",
-        after=(inner,),
+        after=(inner_done,),
     )
     kv_near = shift(kv_own, ROW)
     q_next = shift(q_own, -ROW)
+    kv_far = shift(kv_near, ROW)
+    q_after = shift(q_next, -ROW)
     stat, acc = shape(ROW, 8, TOK, dtype=F32), shape(ROW, AHDIM, TOK, dtype=F32)
     packed = shape(ROW, PACK, TOK)
-    kv_far = shift(kv_near, ROW)
-    q_after = shift(q_next, -ROW)
-    a_stat, a_acc, b_stat, b_acc = call(
+    (a_stat, a_acc, b_stat, b_acc), own_done = call(
         own_kernel, (stat, acc, stat, acc), (), kv_own, q_own, second, name="own", flops=HEAVY
     )
-    n_stat, n_acc = call(
-        next_kernel, (stat, acc), (), q_next, second, name="next", flops=HEAVY, after=(a_stat,)
-    )
-    entering = call(
+    (n_stat, n_acc), next_done = call(
+        next_kernel, (stat, acc), (), q_next, second, name="next", flops=HEAVY, after=(own_done,)
+    )
+    entering, scanned = call(
         scan_kernel,
         shape(owners * 8, 128),
         (),
-        got.reshape(-1, 128),
+        got,
         name="scan",
-        after=(n_stat,),
         scratch=[pltpu.VMEM((owners * 8, 128), F32)] * 2,
+        after=(next_done,),
     )
     came = to_all(entering.reshape(owners, 8, 128)).reshape(owners * 8, 128)
-    after = call(after_kernel, packed, (), q_after, second, name="after", flops=HEAVY, after=(n_stat,))
+    after, _ = call(after_kernel, packed, (), q_after, second, name="after", after=(scanned,))
     after = shift(after, ROW)
-    a_stat, a_acc = call(
-        nearer_kernel, (stat, acc), (0,), row, second, kv_near, a_stat, a_acc, name="nearer", flops=HEAVY
-    )
-    join_send = call(join_kernel, packed, (), n_stat, n_acc, after, name="join", flops=HEAVY, after=(a_stat,))
+    (a_stat, a_acc), near_done = call(
+        nearer_kernel, (stat, acc), (0,), row, second, kv_near, a_stat, a_acc, name="nearer"
+    )
+    mixer_out, mixer_done = call(
+        mixer_kernel,
+        shape(tokens, width, dtype=F32),
+        (),
+        turned,
+        state_out.T,
+        inner,
+        came,
+        name="mixer",
+        scratch=[pltpu.VMEM((owners * 8, 128), F32)],
+    )
+    join_send, joined_done = call(
+        join_kernel,
+        packed,
+        (),
+        n_stat,
+        n_acc,
+        after,
+        name="join",
+        flops=HEAVY,
+        after=(mixer_done, near_done),
+    )
     joined = shift(join_send, ROW)
-    out = call(
+
+    pool_send, _ = call(
+        spot_kernel,
+        shape(owners * later_rows, 128),
+        (0, 1),
+        spot,
+        checkpoint_owner,
+        turned,
+        spot_local,
+        came,
+        later,
+        name="spot",
+        scratch=[
+            pltpu.VMEM((owners * 8, 128), F32),
+            pltpu.VMEM((width, 2 * NSTATE), F32),
+            pltpu.VMEM((width // 2 + 8, 128), F32),
+            pltpu.VMEM((owners * later_rows, 128), F32),
+        ],
+        after=(joined_done,),
+    )
+    later_got = to_all(pool_send.reshape(owners, later_rows, 128)).reshape(-1, 128)
+
+    out, _ = call(
         last_kernel,
         (shape(2 * AHDIM, TOK),) * ROW,
         (0, 1),
@@ -608,10 +677,11 @@
         b_stat,
         b_acc,
         joined,
-        name="last", flops=HEAVY,
+        name="last",
+        flops=HEAVY,
         scratch=[pltpu.VMEM((ROW, 2 * AHDIM, TOK), BF)],
     )
-    attention_out = call(
+    attention_out, _ = call(
         back_kernel,
         shape(TOK, width),
         (0,),
@@ -620,45 +690,20 @@
         name="back",
         scratch=[pltpu.VMEM((width, TOK), BF)],
     )
-
-    mixer_out, pool_send = call(
-        mixer_kernel,
-        (shape(tokens, width, dtype=F32), shape(owners * 8, 128)),
-        (0, 1),
-        spot,
-        checkpoint_owner,
-        turned,
-        state_out,
-        inner,
-        spot_local,
-        came,
-        name="mixer",
-        after=(a_stat,),
+    (cache_pool, state_pool), _ = call(
+        cache_kernel,
+        (shape(owners, block_len, 2, width), shape(1, owners, width // 2, dtype=F32)),
+        (),
+        got,
+        later_got,
+        name="cache",
         scratch=[
-            pltpu.VMEM((owners * 8, 128), F32),
-            pltpu.VMEM((width, 2 * NSTATE), F32),
-            pltpu.VMEM((width // 2 + 8, 128), F32),
+            pltpu.VMEM((owners, rows, 128), F32),
+            pltpu.VMEM((owners, later_rows, 128), F32),
         ],
-    )
-    cache_pool = call(
-        cache_kernel,
-        shape(owners, block_len, 2, width),
-        (),
-        got.reshape(-1, 128),
-        name="cache",
-        scratch=[pltpu.VMEM((owners, 4 * lanes + 8, 128), F32)],
         mib=24,
-        after=(pool_send,),
-    ).reshape(1, owners * block_len, 2, width)
-    pool_got = to_all(pool_send.reshape(owners, 8, 128)).reshape(owners * 8, 128)
-    state_pool = call(
-        pool_kernel,
-        shape(1, owners, width // 2, dtype=F32),
-        (),
-        pool_got,
-        name="pool",
-        scratch=[pltpu.VMEM((owners * 8, 128), F32)],
-    )
+    )
+    cache_pool = cache_pool.reshape(1, owners * block_len, 2, width)
     return (mixer_out, attention_out, state_pool, cache_pool)
 
 

time: 193 us -> 178 us (0.922); the launches traced: 192 us -> 175 us
  waiting for transfers between devices: 57.4 us -> 33.3 us
  local copies, waits for them, and re-layouts: 12.7 us -> 16.8 us
  Pallas kernels: 43.9 us -> 46 us
    all_to_all x3, waiting for transfers between devices: 14.4 us -> 2.36 us  [to_all(): return lax.all_to_all(x, 'seq', split_axis=0, concat_axis=0, tiled=True)]
    ppermute x6, waiting for transfers between devices: 30 us -> 18.7 us  [shift(): lax.ppermute(x, 'seq', [(i - distance, i) for i in devices if i - distanc...]
    unnamed x58 -> x56, local copies, waits for them, and re-layouts: 12.7 us -> 16.8 us
    pallas_call x16, Pallas kernels: 43.9 us -> 46 us  [call(): pl.pallas_call(run, out_shape=out_shapes, in_specs=specs, out_specs=tuple...]
  transfers between devices with their start and end apart: 15 -> 15, of which waited for: 8 -> 8; matrix products, arithmetic and copies ran while one was open for 1% -> 0% of each run, Pallas kernels for 21% -> 23%
where the time goes in v2:
time: 178 us; the launch traced here: 175 us
  starting transfers between devices  76.9 us (43%)
  Pallas kernels  46 us (26%)
  waiting for transfers between devices  33.3 us (19%)
  local copies, waits for them, and re-layouts  16.8 us (9%)
    pallas_call x16, Pallas kernels, call(): pl.pallas_call(run, out_shape=out_shapes, in_specs=specs, out_specs=tuple...  46 us
    all_to_all x3, starting transfers between devices, to_all(): return lax.all_to_all(x, 'seq', split_axis=0, concat_axis=0, tiled=True)  36.5 us
    ppermute x6, starting transfers between devices, shift(): lax.ppermute(x, 'seq', [(i - distance, i) for i in devices if i - distanc...  28.6 us
    ppermute x6, waiting for transfers between devices, shift(): lax.ppermute(x, 'seq', [(i - distance, i) for i in devices if i - distanc...  18.7 us
    unnamed x56, local copies, waits for them, and re-layouts  16.8 us
    ppermute x6, waiting for transfers between devices, in_row(): lax.ppermute(parts[d], 'seq', [(i, i // ROW * ROW + (i + d) % ROW) for i...  12.3 us
    ppermute x6, starting transfers between devices, in_row(): lax.ppermute(parts[d], 'seq', [(i, i // ROW * ROW + (i + d) % ROW) for i...  11.8 us
  transfers between devices with their start and end apart: 15, of which 8 were waited for; matrix products, arithmetic and copies ran while one was open for 0% of the time, Pallas kernels for 23%

profile of v2, /device:TPU:24, one launch (start us, length us, event | category | flops | bytes accessed | tf_op | source)
XLA Modules:
  0.0 174.6 jit_solution(6561619798490001947)
XLA Ops:
  0.7 1.2 copy-done
  1.8 1.2 copy-done.2
  3.0 1.2 copy-done.10
  4.2 2.2 %prep.1 = (bf16[1344,256]{1,0:T(8,128)(2,1)S(1)}, bf16[1344,256]{1,0:T(8,128)(2,1)}, bf16[1344,256]{1,0:T(8,128)(2,1)}, bf16[1344,256]{1,0:T(8,128)(2,1)}, f32[8,128]{1,0:T(8,128)}) custom-call(s32[1]{0:T(128)} %bitcast.6.refs_0_.refs_1_, bf16[256,1792]{1,0:T(8,128)(2,1)S(1)} %copy-done.10, bf16[256,1792]{1,0:T(8,128)(2,1)S(1)} %copy-done, ...), custom_call_target="tpu_custom_call" | custom-call | tf_op jit(solution)/shard_map/prep/pallas_call | solution.py:40
  6.4 1.5 collective-permute-start
  7.9 2.7 %collective-permute-start.1 = (bf16[1344,256]{1,0:T(8,128)(2,1)}, bf16[1344,256]{1,0:T(8,128)(2,1)}, u32[]{:S(2)}, u32[]{:S(2)}) collective-permute-start(bf16[1344,256]{1,0:T(8,128)(2,1)} %get-tuple-element.54), channel_id=1, source_target_pairs={{0,4},{2,6},{4,0},{6,2},{8,12},{10,14},{12,8},{14,10},{16,20},{18,... | collective-permute-start | bytes 2064392 | tf_op jit(solution)/shard_map/ppermute | solution.py:491
  10.7 1.4 collective-permute-start.2
  12.1 0.8 copy-done.16
  12.9 0.8 copy-done.18
  13.6 2.6 %state.1 = (f32[28,256]{1,0:T(8,128)S(1)}, f32[256,28]{1,0:T(8,128)S(1)}, f32[1024,128]{1,0:T(8,128)S(1)}, f32[8,128]{1,0:T(8,128)}) custom-call(bf16[256,1792]{1,0:T(8,128)(2,1)S(1)} %copy-done.4, f32[28,256]{1,0:T(8,128)S(1)} %copy-done.18, bf16[64,256]{1,0:T(8,128)(2,1)S(1)} %bitcast.20), custom_call_target="tpu_custom_call" | custom-call | tf_op jit(solution)/shard_map/state/pallas_call | solution.py:40
  16.2 2.9 %blocks.1 = (bf16[4096,128]{1,0:T(8,128)(2,1)}, bf16[5120,128]{1,0:T(8,128)(2,1)S(1)}, f32[8,128]{1,0:T(8,128)S(1)}) custom-call(s32[1,128]{1,0:T(1,128)S(1)} %copy-done.19, bf16[256,1792]{1,0:T(8,128)(2,1)S(1)} %copy-done.1, bf16[256,1792]{1,0:T(8,128)(2,1)S(1)} %copy-done.3, f32[1024,128]{1,0:T(8,128)S(1)} %get-tuple-element.48.refs_3_), custom_call_target="tpu_custom_call" | custom-call | tf_op jit(solution)/shard_map/blocks/pallas_call | solution.py:40
  19.2 1.1 copy-done.8
  20.2 13.4 %all-to-all-start = ((bf16[128,32,128]{2,1,0:T(8,128)(2,1)}), bf16[128,32,128]{2,1,0:T(8,128)(2,1)S(1)}, u32[]{:S(2)}, u32[]{:S(2)}) async-start(bf16[128,32,128]{2,1,0:T(8,128)(2,1)} %bitcast.4), calls=%async_computation | async-start | bytes 2097152 | tf_op jit(solution)/shard_map/all_to_all | solution.py:485
  34.3 3.6 %inner.1 = (f32[256,1792]{1,0:T(8,128)S(1)}, f32[64,1792]{1,0:T(8,128)S(1)}, f32[8,128]{1,0:T(8,128)S(1)}) custom-call(s32[1]{0:T(128)S(6)} %sub.11.refs_0_, bf16[256,1792]{1,0:T(8,128)(2,1)S(1)} %copy-done.4, f32[28,256]{1,0:T(8,128)S(1)} %get-tuple-element.47.refs_2_, f32[256,28]{1,0:T(8,128)S(1)} %get-tuple-element.46.refs_3_.refs_0_.refs_2_, ...), custom_call_target="tpu_custom_call" | custom-call | tf_op jit(solution)/shard_map/inner/pallas_call | solution.py:40
  37.9 0.0 copy-start.5
  37.9 1.2 copy-done.5
  39.1 0.8 copy-done.13
  39.9 0.0 collective-permute-done.refs_2_
  39.9 5.6 %collective-permute-done.1.refs_3_ = bf16[1344,256]{1,0:T(8,128)(2,1)} collective-permute-done((bf16[1344,256]{1,0:T(8,128)(2,1)}, bf16[1344,256]{1,0:T(8,128)(2,1)}, u32[]{:S(2)}, u32[]{:S(2)}) %collective-permute-start.1) | collective-permute-done | bytes 688160 | tf_op jit(solution)/shard_map/ppermute | solution.py:491
  45.5 0.3 collective-permute-done.2.refs_4_
  45.8 2.6 %gather.1 = (bf16[4,448,256]{2,1,0:T(8,128)(2,1)}, bf16[4,224,256]{2,1,0:T(8,128)(2,1)S(1)}, bf16[4,672,256]{2,1,0:T(8,128)(2,1)S(1)}, f32[8,128]{1,0:T(8,128)}) custom-call(s32[1]{0:T(128)} %bitcast.6.refs_0_.refs_1_, bf16[1344,256]{1,0:T(8,128)(2,1)S(1)} %get-tuple-element.52.refs_1_, bf16[1344,256]{1,0:T(8,128)(2,1)} %collective-permute-done.refs_2_, ...), custom_call_target="tpu_custom_call" | custom-call | tf_op jit(solution)/shard_map/gather/pallas_call | solution.py:40
  48.4 11.2 %collective-permute-start.3 = (bf16[4,224,256]{2,1,0:T(8,128)(2,1)S(1)}, bf16[4,224,256]{2,1,0:T(8,128)(2,1)}, u32[]{:S(2)}, u32[]{:S(2)}) collective-permute-start(bf16[4,224,256]{2,1,0:T(8,128)(2,1)S(1)} %get-tuple-element.57.refs_1_), channel_id=1, source_target_pairs={{8,0},{10,2},{12,4},{14,6},{16,8},{18,10},{20,12},{22,14},{24,16},... | collective-permute-start | bytes 1376264 | tf_op jit(solution)/shard_map/ppermute | solution.py:502
  59.6 1.9 %collective-permute-start.4 = (bf16[4,448,256]{2,1,0:T(8,128)(2,1)}, bf16[4,448,256]{2,1,0:T(8,128)(2,1)}, u32[]{:S(2)}, u32[]{:S(2)}) collective-permute-start(bf16[4,448,256]{2,1,0:T(8,128)(2,1)} %get-tuple-element.59.refs_0_), channel_id=1, source_target_pairs={{0,8},{2,10},{4,12},{6,14},{8,16},{10,18},{12,20},{14,22},{16,24},... | collective-permute-start | bytes 2752520 | tf_op jit(solution)/shard_map/ppermute | solution.py:502
  61.5 4.1 %own.1 = (f32[4,8,256]{2,1,0:T(8,128)S(1)}, f32[4,224,256]{2,1,0:T(8,128)S(1)}, f32[4,8,256]{2,1,0:T(8,128)S(1)}, f32[4,224,256]{2,1,0:T(8,128)S(1)}, f32[8,128]{1,0:T(8,128)S(1)}) custom-call(bf16[4,448,256]{2,1,0:T(8,128)(2,1)} %get-tuple-element.59.refs_0_, bf16[4,224,256]{2,1,0:T(8,128)(2,1)S(1)} %get-tuple-element.57.refs_1_, ...), custom_call_target="tpu_custom_call" | custom-call | flops 40000000000 | tf_op jit(solution)/shard_map/own/pallas_call | solution.py:40
  65.7 0.9 copy-done.11
  66.6 0.9 copy-done.24
  67.5 0.2 collective-permute-done.3.refs_0_
  67.8 6.6 %collective-permute-start.6 = (bf16[4,224,256]{2,1,0:T(8,128)(2,1)}, bf16[4,224,256]{2,1,0:T(8,128)(2,1)S(1)}, u32[]{:S(2)}, u32[]{:S(2)}) collective-permute-start(bf16[4,224,256]{2,1,0:T(8,128)(2,1)} %collective-permute-done.3.refs_0_), channel_id=1, source_target_pairs={{8,0},{10,2},{12,4},{14,6},{16,8},{18,10},{20,12},{22,14},{24,16},... | collective-permute-start | bytes 1376264 | tf_op jit(solution)/shard_map/ppermute | solution.py:502
  74.4 3.6 %next.1 = (f32[4,8,256]{2,1,0:T(8,128)S(1)}, f32[4,224,256]{2,1,0:T(8,128)S(1)}, f32[8,128]{1,0:T(8,128)S(1)}) custom-call(bf16[4,224,256]{2,1,0:T(8,128)(2,1)} %collective-permute-done.3.refs_0_, bf16[4,672,256]{2,1,0:T(8,128)(2,1)S(1)} %get-tuple-element.58.refs_2_.refs_1_, f32[8,128]{1,0:T(8,128)S(1)} %get-tuple-element.60.refs_2_), custom_call_target="tpu_custom_call" | custom-call | flops 40000000000 | tf_op jit(solution)/shard_map/next/pallas_call | solution.py:40
  78.0 0.9 copy-done.26
  79.0 0.0 all-to-all-done
  79.0 1.3 scan.1
  80.3 9.5 %all-to-all-start.1 = ((bf16[128,8,128]{2,1,0:T(8,128)(2,1)}), bf16[128,8,128]{2,1,0:T(8,128)(2,1)S(1)}, u32[]{:S(2)}, u32[]{:S(2)}) async-start(bf16[128,8,128]{2,1,0:T(8,128)(2,1)} %bitcast.7), calls=%async_computation.1 | async-start | bytes 524288 | tf_op jit(solution)/shard_map/all_to_all | solution.py:485
  89.8 0.0 collective-permute-done.6.refs_0_
  89.8 2.4 %after.1 = (bf16[4,240,256]{2,1,0:T(8,128)(2,1)}, f32[8,128]{1,0:T(8,128)}) custom-call(bf16[4,224,256]{2,1,0:T(8,128)(2,1)S(1)} %collective-permute-done.6.refs_0_, bf16[4,672,256]{2,1,0:T(8,128)(2,1)S(1)} %get-tuple-element.58.refs_2_.refs_1_, f32[8,128]{1,0:T(8,128)S(1)} %get-tuple-element.72.refs_2_), custom_call_target="tpu_custom_call" | custom-call | tf_op jit(solution)/shard_map/after/pallas_call | solution.py:40
  92.2 3.4 %collective-permute-start.7 = (bf16[4,240,256]{2,1,0:T(8,128)(2,1)}, bf16[4,240,256]{2,1,0:T(8,128)(2,1)}, u32[]{:S(2)}, u32[]{:S(2)}) collective-permute-start(bf16[4,240,256]{2,1,0:T(8,128)(2,1)} %get-tuple-element.73), channel_id=1, source_target_pairs={{0,8},{2,10},{4,12},{6,14},{8,16},{10,18},{12,20},{14,22},{16,24},... | collective-permute-start | bytes 1474568 | tf_op jit(solution)/shard_map/ppermute | solution.py:502
  95.6 0.0 collective-permute-done.4.refs_2_
  95.6 3.4 %collective-permute-start.5 = (bf16[4,448,256]{2,1,0:T(8,128)(2,1)}, bf16[4,448,256]{2,1,0:T(8,128)(2,1)}, u32[]{:S(2)}, u32[]{:S(2)}) collective-permute-start(bf16[4,448,256]{2,1,0:T(8,128)(2,1)} %collective-permute-done.4.refs_2_), channel_id=1, source_target_pairs={{0,8},{2,10},{4,12},{6,14},{8,16},{10,18},{12,20},{14,22},{16,24},... | collective-permute-start | bytes 2752520 | tf_op jit(solution)/shard_map/ppermute | solution.py:502
  99.0 1.2 copy-done.12
  100.2 3.8 %nearer.1 = (f32[4,8,256]{2,1,0:T(8,128)S(1)}, f32[4,224,256]{2,1,0:T(8,128)S(1)}, f32[8,128]{1,0:T(8,128)S(1)}) custom-call(s32[1]{0:T(128)} %bitcast.9.refs_0_, bf16[4,672,256]{2,1,0:T(8,128)(2,1)S(1)} %get-tuple-element.58.refs_2_.refs_1_, bf16[4,448,256]{2,1,0:T(8,128)(2,1)} %collective-permute-done.4.refs_2_, ...), custom_call_target="tpu_custom_call" | custom-call | tf_op jit(solution)/shard_map/nearer/pallas_call | solution.py:40
  104.0 0.0 copy-start.22
  104.0 0.9 copy-done.22
  104.9 0.0 all-to-all-done.1
  104.9 1.5 copy-done.6
  106.4 3.1 %mixer.1 = (f32[256,1792]{1,0:T(8,128)}, f32[8,128]{1,0:T(8,128)S(1)}) custom-call(f32[256,28]{1,0:T(8,128)S(1)} %get-tuple-element.46.refs_3_.refs_0_.refs_2_, bf16[64,256]{1,0:T(8,128)(2,1)S(1)} %bitcast.19, f32[256,1792]{1,0:T(8,128)S(1)} %copy-done.6, bf16[1024,128]{1,0:T(8,128)(2,1)S(1)} %bitcast.15), custom_call_target="tpu_custom_call" | custom-call | tf_op jit(solution)/shard_map/mixer/pallas_call | solution.py:40
  109.5 1.3 collective-permute-done.7.refs_2_
  110.8 2.2 %join.1 = (bf16[4,240,256]{2,1,0:T(8,128)(2,1)}, f32[8,128]{1,0:T(8,128)S(1)}) custom-call(f32[4,8,256]{2,1,0:T(8,128)S(1)} %get-tuple-element.70.refs_0_, f32[4,224,256]{2,1,0:T(8,128)S(1)} %copy-done.27, bf16[4,240,256]{2,1,0:T(8,128)(2,1)} %collective-permute-done.7.refs_2_, f32[8,128]{1,0:T(8,128)S(1)} %get-tuple-element.74.refs_3_, ...), custom_call_target="tpu_custom_call" | custom-call | flops 40000000000 | tf_op jit(solution)/shard_map/join/pallas_call | solution.py:40
  113.0 2.1 %collective-permute-start.8 = (bf16[4,240,256]{2,1,0:T(8,128)(2,1)}, bf16[4,240,256]{2,1,0:T(8,128)(2,1)}, u32[]{:S(2)}, u32[]{:S(2)}) collective-permute-start(bf16[4,240,256]{2,1,0:T(8,128)(2,1)} %get-tuple-element.76), channel_id=1, source_target_pairs={{0,8},{2,10},{4,12},{6,14},{8,16},{10,18},{12,20},{14,22},{16,24},... | collective-permute-start | bytes 1474568 | tf_op jit(solution)/shard_map/ppermute | solution.py:502
  115.2 2.1 %spot.1 = (bf16[5120,128]{1,0:T(8,128)(2,1)S(1)}, f32[8,128]{1,0:T(8,128)}) custom-call(s32[1]{0:T(128)S(6)} %sub.11.refs_0_, s32[1,128]{1,0:T(1,128)S(1)} %copy-done.21, f32[256,28]{1,0:T(8,128)S(1)} %get-tuple-element.46.refs_3_.refs_0_.refs_2_, f32[64,1792]{1,0:T(8,128)S(1)} %copy-done.14, bf16[1024,128]{1,0:T(8,128)(2,1)S(1)} %bitcast.16, ...), custom_call_target="tpu_custom_call" | custom-call | tf_op jit(solution)/shard_map/spot/pallas_call | solution.py:40
  117.3 1.1 copy-done.7
  118.3 13.6 %all-to-all-start.2 = ((bf16[128,40,128]{2,1,0:T(8,128)(2,1)}), bf16[128,40,128]{2,1,0:T(8,128)(2,1)}, u32[]{:S(2)}, u32[]{:S(2)}) async-start(bf16[128,40,128]{2,1,0:T(8,128)(2,1)} %bitcast.17), calls=%async_computation.2 | async-start | bytes 2621440 | tf_op jit(solution)/shard_map/all_to_all | solution.py:485
  131.9 0.0 collective-permute-done.5.refs_3_
  132.0 17.1 %collective-permute-done.8.refs_8_ = bf16[4,240,256]{2,1,0:T(8,128)(2,1)} collective-permute-done((bf16[4,240,256]{2,1,0:T(8,128)(2,1)}, bf16[4,240,256]{2,1,0:T(8,128)(2,1)}, u32[]{:S(2)}, u32[]{:S(2)}) %collective-permute-start.8) | collective-permute-done | bytes 491552 | tf_op jit(solution)/shard_map/ppermute | solution.py:502
  149.1 1.2 copy-done.25
  150.2 3.8 %last.1 = (bf16[448,256]{1,0:T(8,128)(2,1)S(1)}, bf16[448,256]{1,0:T(8,128)(2,1)S(1)}, bf16[448,256]{1,0:T(8,128)(2,1)S(1)}, bf16[448,256]{1,0:T(8,128)(2,1)S(1)}, f32[8,128]{1,0:T(8,128)}) custom-call(s32[1]{0:T(128)} %bitcast.9.refs_0_, s32[1]{0:T(128)} %bitcast.6.refs_0_.refs_1_, bf16[4,672,256]{2,1,0:T(8,128)(2,1)S(1)} %get-tuple-element.58.refs_2_.refs_1_, ...), custom_call_target="tpu_custom_call" | custom-call | flops 40000000000 | tf_op jit(solution)/shard_map/last/pallas_call | solution.py:40
  154.0 1.4 collective-permute-start.9
  155.4 3.2 %collective-permute-start.10 = (bf16[448,256]{1,0:T(8,128)(2,1)S(1)}, bf16[448,256]{1,0:T(8,128)(2,1)S(1)}, u32[]{:S(2)}, u32[]{:S(2)}) collective-permute-start(bf16[448,256]{1,0:T(8,128)(2,1)S(1)} %get-tuple-element.79), channel_id=1, source_target_pairs={{0,4},{2,6},{4,0},{6,2},{8,12},{10,14},{12,8},{14,10},{16,20},{18,... | collective-permute-start | bytes 688136 | tf_op jit(solution)/shard_map/ppermute | solution.py:491
  158.6 1.5 collective-permute-start.11
  160.1 1.7 collective-permute-done.9.refs_2_
  161.8 4.8 %collective-permute-done.10.refs_3_ = bf16[448,256]{1,0:T(8,128)(2,1)S(1)} collective-permute-done((bf16[448,256]{1,0:T(8,128)(2,1)S(1)}, bf16[448,256]{1,0:T(8,128)(2,1)S(1)}, u32[]{:S(2)}, u32[]{:S(2)}) %collective-permute-start.10) | collective-permute-done | bytes 229408 | tf_op jit(solution)/shard_map/ppermute | solution.py:491
  166.6 0.0 collective-permute-done.11.refs_4_
  166.6 1.3 back.1
  167.9 2.4 %all-to-all-done.2 = bf16[128,40,128]{2,1,0:T(8,128)(2,1)} async-done(((bf16[128,40,128]{2,1,0:T(8,128)(2,1)}), bf16[128,40,128]{2,1,0:T(8,128)(2,1)}, u32[]{:S(2)}, u32[]{:S(2)}) %all-to-all-start.2) | async-done | bytes 1310752 | tf_op jit(solution)/shard_map/all_to_all | solution.py:485
  170.2 4.4 %cache.1 = (bf16[128,2,2,1792]{3,2,1,0:T(2,128)(2,1)}, f32[1,128,896]{2,1,0:T(8,128)}, f32[8,128]{1,0:T(8,128)}) custom-call(bf16[4096,128]{1,0:T(8,128)(2,1)S(1)} %bitcast.14, bf16[5120,128]{1,0:T(8,128)(2,1)} %bitcast.11.refs_1_), custom_call_target="tpu_custom_call" | custom-call | tf_op jit(solution)/shard_map/cache/pallas_call | solution.py:40
  (38 shorter events, 0.1 us)
Async XLA Ops:
  0.6 1.2 copy-start
  1.8 1.2 copy-start.2
  3.0 1.2 copy-start.10
  4.2 7.9 %copy-start.4 = (bf16[256,1792]{1,0:T(8,128)(2,1)S(1)}, bf16[256,1792]{1,0:T(8,128)(2,1)}, u32[]{:S(2)}) copy-start(bf16[256,1792]{1,0:T(8,128)(2,1)} %refs_1_.7) | copy-start | bytes 2752516
  4.2 12.0 %copy-start.1 = (bf16[256,1792]{1,0:T(8,128)(2,1)S(1)}, bf16[256,1792]{1,0:T(8,128)(2,1)}, u32[]{:S(2)}) copy-start(bf16[256,1792]{1,0:T(8,128)(2,1)} %refs_2_.3) | copy-start | bytes 2752516
  4.2 12.0 %copy-start.3 = (bf16[256,1792]{1,0:T(8,128)(2,1)S(1)}, bf16[256,1792]{1,0:T(8,128)(2,1)}, u32[]{:S(2)}) copy-start(bf16[256,1792]{1,0:T(8,128)(2,1)} %refs_3_.1) | copy-start | bytes 2752516
  4.2 12.0 %copy-start.19 = (s32[1,128]{1,0:T(1,128)S(1)}, s32[1,128]{1,0:T(1,128)}, u32[]{:S(2)}) copy-start(s32[1,128]{1,0:T(1,128)} %refs_0_.3) | copy-start | bytes 1540
  6.4 33.5 %collective-permute-start = (bf16[1344,256]{1,0:T(8,128)(2,1)}, bf16[1344,256]{1,0:T(8,128)(2,1)}, u32[]{:S(2)}, u32[]{:S(2)}) collective-permute-start(bf16[1344,256]{1,0:T(8,128)(2,1)} %get-tuple-element.53), channel_id=1, source_target_pairs={{0,2},{2,4},{4,6},{6,0},{8,10},{10,12},{12,14},{14,8},{16,18},{18,... | collective-permute-start | bytes 2064392 | tf_op jit(solution)/shard_map/ppermute | solution.py:491
  7.9 37.6 %collective-permute-start.1 = (bf16[1344,256]{1,0:T(8,128)(2,1)}, bf16[1344,256]{1,0:T(8,128)(2,1)}, u32[]{:S(2)}, u32[]{:S(2)}) collective-permute-start(bf16[1344,256]{1,0:T(8,128)(2,1)} %get-tuple-element.54), channel_id=1, source_target_pairs={{0,4},{2,6},{4,0},{6,2},{8,12},{10,14},{12,8},{14,10},{16,20},{18,... | collective-permute-start | bytes 2064392 | tf_op jit(solution)/shard_map/ppermute | solution.py:491
  10.7 35.1 %collective-permute-start.2 = (bf16[1344,256]{1,0:T(8,128)(2,1)}, bf16[1344,256]{1,0:T(8,128)(2,1)}, u32[]{:S(2)}, u32[]{:S(2)}) collective-permute-start(bf16[1344,256]{1,0:T(8,128)(2,1)} %get-tuple-element.55), channel_id=1, source_target_pairs={{0,6},{2,0},{4,2},{6,4},{8,14},{10,8},{12,10},{14,12},{16,22},{18,... | collective-permute-start | bytes 2064392 | tf_op jit(solution)/shard_map/ppermute | solution.py:491
  12.1 0.8 copy-start.16
  12.8 0.8 copy-start.18
  19.2 1.1 copy-start.8
  20.2 14.0 %copy-start.15 = (bf16[256,64]{0,1:T(8,128)(2,1)S(1)}, bf16[256,64]{0,1:T(8,128)(2,1)}, u32[]{:S(2)}) copy-start(bf16[256,64]{0,1:T(8,128)(2,1)} %param.14) | copy-start | bytes 98308
  20.2 14.0 %copy-start.17 = (bf16[256,64]{0,1:T(8,128)(2,1)S(1)}, bf16[256,64]{0,1:T(8,128)(2,1)}, u32[]{:S(2)}) copy-start(bf16[256,64]{0,1:T(8,128)(2,1)} %param.13) | copy-start | bytes 98308
  20.2 14.0 %copy-start.20 = (f32[28]{0:T(128)S(1)}, f32[28]{0:T(128)}, u32[]{:S(2)}) copy-start(f32[28]{0:T(128)} %param.15) | copy-start | bytes 340
  20.2 58.7 %all-to-all-start = ((bf16[128,32,128]{2,1,0:T(8,128)(2,1)}), bf16[128,32,128]{2,1,0:T(8,128)(2,1)S(1)}, u32[]{:S(2)}, u32[]{:S(2)}) async-start(bf16[128,32,128]{2,1,0:T(8,128)(2,1)} %bitcast.4), calls=%async_computation | async-start | bytes 2097152 | tf_op jit(solution)/shard_map/all_to_all | solution.py:485
  37.9 1.2 copy-start.5
  39.1 0.8 copy-start.13
  48.4 19.4 %collective-permute-start.3 = (bf16[4,224,256]{2,1,0:T(8,128)(2,1)S(1)}, bf16[4,224,256]{2,1,0:T(8,128)(2,1)}, u32[]{:S(2)}, u32[]{:S(2)}) collective-permute-start(bf16[4,224,256]{2,1,0:T(8,128)(2,1)S(1)} %get-tuple-element.57.refs_1_), channel_id=1, source_target_pairs={{8,0},{10,2},{12,4},{14,6},{16,8},{18,10},{20,12},{22,14},{24,16},... | collective-permute-start | bytes 1376264 | tf_op jit(solution)/shard_map/ppermute | solution.py:502
  59.6 36.0 %collective-permute-start.4 = (bf16[4,448,256]{2,1,0:T(8,128)(2,1)}, bf16[4,448,256]{2,1,0:T(8,128)(2,1)}, u32[]{:S(2)}, u32[]{:S(2)}) collective-permute-start(bf16[4,448,256]{2,1,0:T(8,128)(2,1)} %get-tuple-element.59.refs_0_), channel_id=1, source_target_pairs={{0,8},{2,10},{4,12},{6,14},{8,16},{10,18},{12,20},{14,22},{16,24},... | collective-permute-start | bytes 2752520 | tf_op jit(solution)/shard_map/ppermute | solution.py:502
  65.6 1.0 copy-start.11
  66.6 0.9 copy-start.24
  67.8 22.0 %collective-permute-start.6 = (bf16[4,224,256]{2,1,0:T(8,128)(2,1)}, bf16[4,224,256]{2,1,0:T(8,128)(2,1)S(1)}, u32[]{:S(2)}, u32[]{:S(2)}) collective-permute-start(bf16[4,224,256]{2,1,0:T(8,128)(2,1)} %collective-permute-done.3.refs_0_), channel_id=1, source_target_pairs={{8,0},{10,2},{12,4},{14,6},{16,8},{18,10},{20,12},{22,14},{24,16},... | collective-permute-start | bytes 1376264 | tf_op jit(solution)/shard_map/ppermute | solution.py:502
  78.0 1.0 copy-start.26
  80.3 24.6 %all-to-all-start.1 = ((bf16[128,8,128]{2,1,0:T(8,128)(2,1)}), bf16[128,8,128]{2,1,0:T(8,128)(2,1)S(1)}, u32[]{:S(2)}, u32[]{:S(2)}) async-start(bf16[128,8,128]{2,1,0:T(8,128)(2,1)} %bitcast.7), calls=%async_computation.1 | async-start | bytes 524288 | tf_op jit(solution)/shard_map/all_to_all | solution.py:485
  92.2 18.6 %collective-permute-start.7 = (bf16[4,240,256]{2,1,0:T(8,128)(2,1)}, bf16[4,240,256]{2,1,0:T(8,128)(2,1)}, u32[]{:S(2)}, u32[]{:S(2)}) collective-permute-start(bf16[4,240,256]{2,1,0:T(8,128)(2,1)} %get-tuple-element.73), channel_id=1, source_target_pairs={{0,8},{2,10},{4,12},{6,14},{8,16},{10,18},{12,20},{14,22},{16,24},... | collective-permute-start | bytes 1474568 | tf_op jit(solution)/shard_map/ppermute | solution.py:502
  95.6 36.4 %collective-permute-start.5 = (bf16[4,448,256]{2,1,0:T(8,128)(2,1)}, bf16[4,448,256]{2,1,0:T(8,128)(2,1)}, u32[]{:S(2)}, u32[]{:S(2)}) collective-permute-start(bf16[4,448,256]{2,1,0:T(8,128)(2,1)} %collective-permute-done.4.refs_2_), channel_id=1, source_target_pairs={{0,8},{2,10},{4,12},{6,14},{8,16},{10,18},{12,20},{14,22},{16,24},... | collective-permute-start | bytes 2752520 | tf_op jit(solution)/shard_map/ppermute | solution.py:502
  99.0 1.2 copy-start.12
  104.0 0.9 copy-start.22
  104.9 1.5 copy-start.6
  106.4 4.4 %copy-start.27 = (f32[4,224,256]{2,1,0:T(8,128)S(1)}, f32[4,224,256]{2,1,0:T(8,128)}, u32[]{:S(2)}) copy-start(f32[4,224,256]{2,1,0:T(8,128)} %copy-done.26) | copy-start | bytes 2752516
  110.8 4.4 %copy-start.9 = (bf16[5120,128]{1,0:T(8,128)(2,1)S(1)}, bf16[5120,128]{1,0:T(8,128)(2,1)}, u32[]{:S(2)}) copy-start(bf16[5120,128]{1,0:T(8,128)(2,1)} %copy-done.8) | copy-start | bytes 3932164
  110.8 4.4 %copy-start.14 = (f32[64,1792]{1,0:T(8,128)S(1)}, f32[64,1792]{1,0:T(8,128)}, u32[]{:S(2)}) copy-start(f32[64,1792]{1,0:T(8,128)} %copy-done.13) | copy-start | bytes 1376260
  110.8 4.4 %copy-start.21 = (s32[1,128]{1,0:T(1,128)S(1)}, s32[1,128]{1,0:T(1,128)}, u32[]{:S(2)}) copy-start(s32[1,128]{1,0:T(1,128)} %refs_1_.9) | copy-start | bytes 1540
  113.0 36.0 %collective-permute-start.8 = (bf16[4,240,256]{2,1,0:T(8,128)(2,1)}, bf16[4,240,256]{2,1,0:T(8,128)(2,1)}, u32[]{:S(2)}, u32[]{:S(2)}) collective-permute-start(bf16[4,240,256]{2,1,0:T(8,128)(2,1)} %get-tuple-element.76), channel_id=1, source_target_pairs={{0,8},{2,10},{4,12},{6,14},{8,16},{10,18},{12,20},{14,22},{16,24},... | collective-permute-start | bytes 1474568 | tf_op jit(solution)/shard_map/ppermute | solution.py:502
  117.3 1.1 copy-start.7
  118.3 30.7 %copy-start.23 = (f32[4,224,256]{2,1,0:T(8,128)S(1)}, f32[4,224,256]{2,1,0:T(8,128)}, u32[]{:S(2)}) copy-start(f32[4,224,256]{2,1,0:T(8,128)} %copy-done.22) | copy-start | bytes 2752516
  118.3 51.9 %all-to-all-start.2 = ((bf16[128,40,128]{2,1,0:T(8,128)(2,1)}), bf16[128,40,128]{2,1,0:T(8,128)(2,1)}, u32[]{:S(2)}, u32[]{:S(2)}) async-start(bf16[128,40,128]{2,1,0:T(8,128)(2,1)} %bitcast.17), calls=%async_computation.2 | async-start | bytes 2621440 | tf_op jit(solution)/shard_map/all_to_all | solution.py:485
  149.1 1.2 copy-start.25
  154.0 7.8 %collective-permute-start.9 = (bf16[448,256]{1,0:T(8,128)(2,1)S(1)}, bf16[448,256]{1,0:T(8,128)(2,1)S(1)}, u32[]{:S(2)}, u32[]{:S(2)}) collective-permute-start(bf16[448,256]{1,0:T(8,128)(2,1)S(1)} %get-tuple-element.78), channel_id=1, source_target_pairs={{0,2},{2,4},{4,6},{6,0},{8,10},{10,12},{12,14},{14,8},{16,18},{18,... | collective-permute-start | bytes 688136 | tf_op jit(solution)/shard_map/ppermute | solution.py:491
  155.4 11.1 %collective-permute-start.10 = (bf16[448,256]{1,0:T(8,128)(2,1)S(1)}, bf16[448,256]{1,0:T(8,128)(2,1)S(1)}, u32[]{:S(2)}, u32[]{:S(2)}) collective-permute-start(bf16[448,256]{1,0:T(8,128)(2,1)S(1)} %get-tuple-element.79), channel_id=1, source_target_pairs={{0,4},{2,6},{4,0},{6,2},{8,12},{10,14},{12,8},{14,10},{16,20},{18,... | collective-permute-start | bytes 688136 | tf_op jit(solution)/shard_map/ppermute | solution.py:491
  158.6 7.9 %collective-permute-start.11 = (bf16[448,256]{1,0:T(8,128)(2,1)S(1)}, bf16[448,256]{1,0:T(8,128)(2,1)S(1)}, u32[]{:S(2)}, u32[]{:S(2)}) collective-permute-start(bf16[448,256]{1,0:T(8,128)(2,1)S(1)} %get-tuple-element.80), channel_id=1, source_target_pairs={{0,6},{2,0},{4,2},{6,4},{8,14},{10,8},{12,10},{14,12},{16,22},{18,... | collective-permute-start | bytes 688136 | tf_op jit(solution)/shard_map/ppermute | solution.py:491
